TPU v7x, 512 devices: a whole 4x8x8 slice. The times are simulated.
512 devices in a mesh: src: 32 (over z, x), rcv: 16 (over y, core).
Axes of the slice: x: 4, y: 8, z: 8, core: 2. Of those that a mesh axis runs over, the one named last changes fastest.
Arguments:
- stiffness: bfloat16 [2, 131072, 2048], P(None, 'src', 'rcv'), may hold values from -0.046875 to 0.046875
- newton_rhs: float32 [48, 2, 131072], P(None, None, ('src', 'rcv')), may hold values from -6 to 6
- traction: float32 [48, 2, 2048], P(None, None, 'rcv'), may hold values from -8 to 8
- opening: float32 [48, 2048], P(None, 'rcv'), may hold values from -6 to 6
- state: int32 [48, 2048], P(None, 'rcv'), may hold values from 0 to 2
- elements: int32 [2048], P('rcv'), may hold values from 0 to 131071, as said below
Outputs:
- increment: float32 [48, 2, 131072], P(None, None, ('src', 'rcv'))
- residual: float32 [48, 2, 131072], P(None, None, ('src', 'rcv'))
Inputs may be any that keep to these rules, and one draw needn't show every extreme that they name: 2048 distinct source elements, including 0 and 131071. `state`: 0 sticking, 1 slipping, 2 open.
All inputs are finite; a program needn't handle non-finite values.
Results may differ from a plain program's by a relative error of at most 0.012.
The roundings to bfloat16 on the way count: a program that leaves them out, or rounds other values in their place, can miss the bound.
Values may be sent and summed in bfloat16 or wider, within the bound.
A program may use at most 64 MiB of HBM per device.

v0:
```python
import jax
import jax.numpy as jnp
from jax import lax
from jax.sharding import PartitionSpec as P

ITERS = 2


def coefficients(traction, opening, state):
    tau = traction[:, 0, :]
    press = traction[:, 1, :]
    radius = jnp.sqrt(opening * opening + press * press + 0.5)
    a_normal = 1.0 - opening / radius
    b_normal = 1.0 - press / radius
    ratio = jnp.abs(tau) / (1.0 + 0.6 * jnp.abs(press))
    a_shear = jnp.where(state == 0, 1.0, jnp.where(state == 1, ratio, 0.0))
    b_shear = jnp.where(state == 0, ratio, 1.0)
    coef_a = jnp.stack([a_shear, a_normal], axis=1)
    coef_b = jnp.stack([b_shear, b_normal], axis=1)
    return (coef_a, coef_b)


def shards(stiffness, newton_rhs, traction, opening, state, elements):
    block_len = stiffness.shape[1]
    local_index = elements - lax.axis_index("src") * block_len
    inside_block = (local_index >= 0) & (local_index < block_len)
    drop_index = jnp.where(inside_block, local_index, block_len)
    coef_a, coef_b = coefficients(traction, opening, state)

    def square_sum(vector):
        return lax.psum(jnp.sum(vector * vector, axis=(1, 2)), ("src", "rcv"))

    residual = newton_rhs
    increment = jnp.zeros_like(residual)
    direction = residual
    norm_now = square_sum(residual)
    for step in range(ITERS):
        apply_vb = direction.astype(jnp.bfloat16)
        piece = lax.all_gather(apply_vb, "rcv", axis=2, tiled=True)
        count = piece.shape[2]
        kd_sum = jnp.einsum("bcs,csr->bcr", piece, stiffness, preferred_element_type=jnp.float32)
        within = (local_index >= 0) & (local_index < count)
        picked = jnp.take(piece, jnp.clip(local_index, 0, count - 1), axis=2)
        ed_sum = jnp.where(within, picked.astype(jnp.float32), 0.0)
        jv = lax.psum(coef_a * ed_sum + coef_b * kd_sum, "src")
        weighted = (coef_b * jv).astype(jnp.bfloat16)
        lifted = coef_a * jv
        term = jnp.einsum("bcr,csr->bcs", weighted, stiffness, preferred_element_type=jnp.float32)
        term = term.at[:, :, drop_index].add(lifted, mode="drop")
        summed = lax.psum_scatter(term, "rcv", scatter_dimension=2, tiled=True)
        image = summed + 0.5 * direction
        own_dir = direction
        curve = lax.psum(jnp.sum(own_dir * image, axis=(1, 2)), ("src", "rcv"))
        alpha = norm_now / curve
        increment = increment + alpha[:, None, None] * direction
        residual = residual - alpha[:, None, None] * image
        norm_next = square_sum(residual)
        direction = residual + (norm_next / norm_now)[:, None, None] * direction
        norm_now = norm_next
    return (increment, residual)


def solution(mesh):
    placed = (
        P(None, "src", "rcv"),
        P(None, None, ("src", "rcv")),
        P(None, None, "rcv"),
        P(None, "rcv"),
        P(None, "rcv"),
        P("rcv"),
    )
    return jax.shard_map(
        shards,
        mesh=mesh,
        in_specs=placed,
        out_specs=(P(None, None, ("src", "rcv")), P(None, None, ("src", "rcv"))),
        check_vma=False,
    )
```

profile of v0, /device:TPU:1, one launch (start us, length us, event | category | flops | bytes accessed | tf_op | source)
XLA Modules:
  0.0 821.4 jit_solution(13842991310198974770)
XLA Ops:
  7.2 0.0 copy-start
  7.2 0.0 copy-start.4
  7.2 0.0 copy-start.3
  7.2 0.0 reduce-scatter.3.cloned.1.call-start
  7.2 1.0 fusion.7
  8.3 0.7 compare_and_fusion
  8.9 0.9 copy.65
  9.8 23.5 %all_gather.6 = bf16[48,2,4096]{2,0,1:T(8,128)(2,1)S(1)} all-gather(bf16[48,2,256]{2,0,1:T(8,128)(2,1)S(1)} %copy.65), channel_id=1, replica_groups=mesh['src'=32,'rcv'=16] {'rcv'}, dimensions={2}, use_global_device_ids=true | all-gather | bytes 835584 | tf_op jit(solution)/shard_map/all_gather | solution.py:39
  33.4 3.8 copy.27
  37.2 2.3 gather_fusion
  39.5 0.1 copy.28
  39.6 0.0 copy-done.4
  39.7 0.0 copy-done
  39.7 0.5 fusion.1
  40.2 0.0 copy-start.5
  40.2 118.9 %psum.43 = f32[48,2,128]{2,0,1:T(8,128)S(1)} all-reduce(f32[48,2,128]{2,0,1:T(8,128)S(1)} %fusion.1), channel_id=1, replica_groups=mesh['src'=32,'rcv'=16] {'src'}, use_global_device_ids=true, to_apply=%region_2.4 | all-reduce | flops 12288 | bytes 98304 | tf_op jit(solution)/shard_map/psum | solution.py:45
  159.1 2.0 convolution_bitcast_fusion.1
  161.2 6.1 copy.29
  167.2 0.1 copy.30
  167.3 13.8 %scatter_fusion = f32[48,2,4096]{0,1,2:T(2,128)} fusion(f32[48,2,4096]{0,1,2:T(2,128)} %copy.29, s32[128]{0:T(128)S(1)} %compare_select_fusion.1, f32[128,48,2]{1,2,0:T(2,128)S(1)} %copy.30), kind=kCustom, calls=%fused_computation.2 | custom fusion | flops 12288 | bytes 147968 | tf_op jit(solution)/shard_map/scatter-add | solution.py:49
  181.2 6.2 copy.31
  187.4 0.0 reduce-scatter.3.cloned.1.call-update
  187.4 0.0 reduce-scatter.5.cloned.1.call-start
  187.5 0.4 multiply_reduce_fusion.3
  187.9 77.0 %reduce-scatter.3.cloned.1.call-done = f32[48,2,256]{2,0,1:T(8,128)} async-done(((f32[48,2,4096]{2,0,1:T(8,128)}), f32[48,2,256]{2,0,1:T(8,128)}) %reduce-scatter.3.cloned.1.call-update) | async-done | bytes 98320 | tf_op jit(solution)/shard_map/reduce_scatter | solution.py:50
  265.0 1.0 multiply_reduce_fusion.2
  266.0 100.0 %all-reduce = (f32[48]{0:T(128)S(1)}, f32[48]{0:T(128)S(1)}) all-reduce(f32[48]{0:T(128)S(1)} %multiply_reduce_fusion.3, f32[48]{0:T(128)S(1)} %multiply_reduce_fusion.2), channel_id=1, replica_groups=mesh['src'=32,'rcv'=16] {'src','rcv'}, use_global_device_ids=true, to_apply=%region_1.2 | all-reduce | flops 96 | bytes 768 | tf_op jit(solution)/shard_map/psum | solution.py:31
  366.0 1.1 multiply_reduce_fusion.1
  367.1 94.4 %psum.45 = f32[48]{0:T(128)S(1)} all-reduce(f32[48]{0:T(128)S(1)} %multiply_reduce_fusion.1), channel_id=1, replica_groups=mesh['src'=32,'rcv'=16] {'src','rcv'}, use_global_device_ids=true, to_apply=%region_8.10 | all-reduce | flops 48 | bytes 384 | tf_op jit(solution)/shard_map/psum | solution.py:31
  461.5 1.0 fusion.6
  462.5 18.1 %all_gather.7 = bf16[48,2,4096]{2,0,1:T(8,128)(2,1)S(1)} all-gather(bf16[48,2,256]{2,0,1:T(8,128)(2,1)S(1)} %fusion.6), channel_id=1, replica_groups=mesh['src'=32,'rcv'=16] {'rcv'}, dimensions={2}, use_global_device_ids=true | all-gather | bytes 835584 | tf_op jit(solution)/shard_map/all_gather | solution.py:39
  480.6 3.8 copy.37
  484.4 2.3 gather_fusion.1
  486.8 0.1 copy.38
  486.9 0.5 fusion.3
  487.3 112.6 %psum.46 = f32[48,2,128]{2,0,1:T(8,128)S(1)} all-reduce(f32[48,2,128]{2,0,1:T(8,128)S(1)} %fusion.3), channel_id=1, replica_groups=mesh['src'=32,'rcv'=16] {'src'}, use_global_device_ids=true, to_apply=%region_9.11 | all-reduce | flops 12288 | bytes 98304 | tf_op jit(solution)/shard_map/psum | solution.py:45
  600.0 2.0 convolution_bitcast_fusion
  602.0 6.1 copy.39
  608.0 0.1 copy.40
  608.2 13.8 %scatter_fusion.1 = f32[48,2,4096]{0,1,2:T(2,128)} fusion(f32[48,2,4096]{0,1,2:T(2,128)} %copy.39, s32[128]{0:T(128)S(1)} %compare_select_fusion.1, f32[128,48,2]{1,2,0:T(2,128)S(1)} %copy.40), kind=kCustom, calls=%fused_computation.3 | custom fusion | flops 12288 | bytes 147968 | tf_op jit(solution)/shard_map/scatter-add | solution.py:49
  622.0 6.2 copy.41
  628.2 0.0 reduce-scatter.5.cloned.1.call-update
  628.3 82.8 %reduce-scatter.5.cloned.1.call-done = f32[48,2,256]{2,0,1:T(8,128)} async-done(((f32[48,2,4096]{2,0,1:T(8,128)}), f32[48,2,256]{2,0,1:T(8,128)}) %reduce-scatter.5.cloned.1.call-update) | async-done | bytes 98320 | tf_op jit(solution)/shard_map/reduce_scatter | solution.py:50
  711.0 1.1 multiply_reduce_fusion
  712.1 100.0 %psum.47 = f32[48]{0:T(128)S(1)} all-reduce(f32[48]{0:T(128)S(1)} %multiply_reduce_fusion), channel_id=1, replica_groups=mesh['src'=32,'rcv'=16] {'src','rcv'}, use_global_device_ids=true, to_apply=%region_13.15 | all-reduce | flops 48 | bytes 384 | tf_op jit(solution)/shard_map/psum | solution.py:53
  812.1 1.0 multiply_subtract_fusion
  813.1 0.7 copy.42
  813.9 0.7 copy.43
  (14 shorter events, 0.1 us)
Async XLA Ops:
  7.2 32.5 %copy-start = (bf16[2,4096,128]{2,1,0:T(8,128)(2,1)S(1)}, bf16[2,4096,128]{2,1,0:T(8,128)(2,1)}, u32[]{:S(2)}) copy-start(bf16[2,4096,128]{2,1,0:T(8,128)(2,1)} %param.8) | copy-start | bytes 6291460
  7.2 32.5 %copy-start.4 = (f32[48,128]{1,0:T(8,128)S(1)}, f32[48,128]{1,0:T(8,128)}, u32[]{:S(2)}) copy-start(f32[48,128]{1,0:T(8,128)} %param.11) | copy-start | bytes 73732
  7.2 32.5 %copy-start.3 = (s32[48,128]{1,0:T(8,128)S(1)}, s32[48,128]{1,0:T(8,128)}, u32[]{:S(2)}) copy-start(s32[48,128]{1,0:T(8,128)} %param.12) | copy-start | bytes 73732
  7.2 257.8 %reduce-scatter.3.cloned.1.call-start = ((), (), s32[]{:S(2)}) async-start(), calls=%async_computation.2 | async-start | bytes 1671168 | tf_op jit(solution)/shard_map/reduce_scatter | solution.py:50
  40.2 121.0 %copy-start.5 = (s32[128]{0:T(128)S(1)}, s32[128]{0:T(128)}, u32[]{:S(2)}) copy-start(s32[128]{0:T(128)} %param.13) | copy-start | bytes 1540
  181.2 6.3 copy-start.1
  187.4 523.6 %reduce-scatter.5.cloned.1.call-start = ((), (), s32[]{:S(2)}) async-start(), calls=%async_computation.3 | async-start | bytes 1671168 | tf_op jit(solution)/shard_map/reduce_scatter | solution.py:50
  622.0 89.0 %copy-start.2 = (f32[48,2,256]{2,0,1:T(8,128)S(1)}, f32[48,2,256]{2,0,1:T(8,128)}, u32[]{:S(2)}) copy-start(f32[48,2,256]{2,0,1:T(8,128)} %reduce-scatter.3.cloned.1.call-done) | copy-start | bytes 294916
Sparse Core Ops, SparseCore 0:
  187.6 77.3 reduce-scatter.2
  628.4 82.5 reduce-scatter.4
where the time goes:
time: 823 us; the launch traced here: 821 us
  blocking collectives  568 us (69%)
  waiting for transfers between devices  160 us (19%)
  local copies, waits for them, and re-layouts  40.7 us (5%)
  other arithmetic  34 us (4%)
  between operations  14.2 us (2%)
    psum x2, blocking collectives, shards(): jv = lax.psum(coef_a * ed_sum + coef_b * kd_sum, 'src')  232 us
    psum x2, blocking collectives, square_sum(): return lax.psum(jnp.sum(vector * vector, axis=(1, 2)), ('src', 'rcv'))  194 us
    reduce_scatter x2, waiting for transfers between devices, shards(): summed = lax.psum_scatter(term, 'rcv', scatter_dimension=2, tiled=True)  160 us
    psum x1, blocking collectives, shards(): curve = lax.psum(jnp.sum(own_dir * image, axis=(1, 2)), ('src', 'rcv'))  100 us
    all_gather x2, blocking collectives, shards(): piece = lax.all_gather(apply_vb, 'rcv', axis=2, tiled=True)  41.6 us
    scatter-add x2, other arithmetic, shards(): term = term.at[:, :, drop_index].add(lifted, mode='drop')  27.7 us
  transfers between devices with their start and end apart: 2, of which 2 were waited for; matrix products, arithmetic and copies ran while one was open for 0% of the time, Pallas kernels for 0%

commit v1 on v0

v1 whole, which is shorter than its diff:
```python
import jax
import jax.numpy as jnp
from jax import lax
from jax.experimental import pallas as pl
from jax.experimental.pallas import tpu as pltpu
from jax.sharding import PartitionSpec as P

MESH = pl.DeviceIdType.MESH
F32 = jnp.float32
BF16 = jnp.bfloat16
B = 48
L = 256
NY = 8
N_RCV = 16
N_SRC = 32
TILES = 13


def dot_nt(a, b):
    return lax.dot_general(a, b, (((1,), (1,)), ((), ())), preferred_element_type=F32)


def kernel(k_hbm, g_hbm, tr_hbm, op_hbm, st_hbm, el_hbm, x_hbm, r_hbm,
           g_ref, tr_ref, op_ref, st_ref, el_ref, x_ref, r_ref,
           kw, low, elb, co, co_send, sb, gat, acc, j0, ar_s, ar_in, ar_out,
           rs_send, rs_in, rs_fin, own, sib, p_ref, tb,
           k_sem, in_sem, out_sem, sib_send, sib_recv, kp_send, kp_recv, ag_send, ag_recv, rs_ssem, rs_recv, rf_recv,
           sp_send, sp_recv, a1_send, a1_recv, a2_send, a2_recv, t_send, t_recv):
    src = lax.axis_index("src")
    rcv = lax.axis_index("rcv")
    y = rcv // 2
    c = lax.rem(rcv, 2)
    other = 1 - c

    def chip(d):
        return lax.rem(y + d + NY, NY)

    def at_chip(d, core):
        return (src, chip(d) * 2 + core)

    def remote(s, d, ss, rs, dev):
        return pltpu.make_async_remote_copy(
            src_ref=s, dst_ref=d, send_sem=ss, recv_sem=rs, device_id=dev, device_id_type=MESH)

    here = (src, y * 2 + other)

    def wait_recv(ref, sem):
        remote(ref, ref, sem, sem, here).wait_recv()

    def wait_send(ref, sem):
        remote(ref, ref, sem, sem, here).wait_send()

    barrier = pltpu.get_barrier_semaphore()

    def greet(dev):
        pl.semaphore_signal(barrier, inc=1, device_id=dev, device_id_type=MESH)

    def greet_rcv(d, carry):
        greet((src, lax.rem(rcv + d, N_RCV)))
        return carry

    def greet_src(d, carry):
        greet((lax.rem(src + d, N_SRC), rcv))
        return carry

    lax.fori_loop(1, N_RCV, greet_rcv, 0)
    lax.fori_loop(1, N_SRC, greet_src, 0)

    loads = [
        pltpu.make_async_copy(a, b, in_sem.at[i])
        for i, (a, b) in enumerate((
            (g_hbm, g_ref), (tr_hbm, tr_ref), (op_hbm, op_ref), (st_hbm, st_ref), (el_hbm, el_ref)))
    ]
    for load in loads:
        load.start()
    k_copy = pltpu.make_async_copy(k_hbm.at[c], kw.at[c], k_sem)
    k_copy.start()

    lane = lax.broadcasted_iota(jnp.int32, (B, 128), 1)
    case = lax.broadcasted_iota(jnp.int32, (B, 128), 0)
    diag = lane == case

    def row_of(v):
        col = jnp.sum(v, axis=1, keepdims=True)
        return jnp.sum(jnp.where(diag, col, 0.0), axis=0, keepdims=True)

    def col_of(row):
        return jnp.sum(jnp.where(diag, row, 0.0), axis=1, keepdims=True)

    def stage(it, v0, v1):
        b0, b1 = v0.astype(BF16), v1.astype(BF16)
        sb[it, 0] = b0
        sb[it, 1] = b1
        gat[it, rcv] = jnp.where(c == 0, b0, b1)

    loads[0].wait()
    g0, g1 = g_ref[:, 0, :], g_ref[:, 1, :]
    stage(0, g0, g1)
    gg_row = row_of(g0 * g0 + g1 * g1)

    for load in loads[1:]:
        load.wait()
    tau, press = tr_ref[:, 0, :], tr_ref[:, 1, :]
    opening, state = op_ref[...], st_ref[...]
    radius = jnp.sqrt(opening * opening + press * press + 0.5)
    a_n = 1.0 - opening / radius
    b_n = 1.0 - press / radius
    ratio = jnp.abs(tau) / (1.0 + 0.6 * jnp.abs(press))
    a_s = jnp.where(state == 0, 1.0, jnp.where(state == 1, ratio, 0.0))
    b_s = jnp.where(state == 0, ratio, 1.0)
    co[c, 0] = jnp.where(c == 0, a_s, a_n)
    co[c, 1] = jnp.where(c == 0, b_s, b_n)
    co_send[0] = jnp.where(c == 0, a_n, a_s)
    co_send[1] = jnp.where(c == 0, b_n, b_s)
    elb[c, :8, :] = jnp.broadcast_to(el_ref[...], (8, 128))
    pl.semaphore_wait(barrier, N_RCV + N_SRC - 2)

    def gather_start(it):
        for comp in range(2):
            for d in (2, -2, 1, -1):
                remote(sb.at[it, comp], gat.at[it, rcv], ag_send.at[it], ag_recv.at[it, rcv], at_chip(d, comp)).start()
        remote(sb.at[it, other], gat.at[it, rcv], ag_send.at[it], ag_recv.at[it, rcv], here).start()

    def share_k(d):
        q = chip(d)
        rows = pl.ds(pl.multiple_of(q * (2 * L), 2 * L), 2 * L)
        remote(k_hbm.at[other, rows], kw.at[c, rows], kp_send, kp_recv.at[q], here).start()

    def arrived(it, d, h):
        slot = chip(d) * 2 + h
        wait_recv(gat.at[it, slot], ag_recv.at[it, slot])

    def relay(it):
        for d in (1, -1):
            for h in range(2):
                arrived(it, -2 * d, h)
                slot = chip(-2 * d) * 2 + h
                part = gat.at[it, slot]
                if (d == 1) == (h == 0):
                    remote(part, part, ag_send.at[it], ag_recv.at[it, slot], at_chip(2 * d, c)).start()
                remote(part, part, ag_send.at[it], ag_recv.at[it, slot], at_chip(d, c)).start()

    def block(q):
        rows = pl.ds(pl.multiple_of(q * (2 * L), 2 * L), 2 * L)
        return jnp.concatenate([kw[0, rows, :], kw[1, rows, :]], axis=1)

    def add_chip(it, d):
        q = chip(d)
        if it == 0:
            rows = pl.ds(pl.multiple_of(q * (2 * L), 2 * L), 2 * L)
            wait_recv(kw.at[other, rows], kp_recv.at[q])
        v0, v1 = gat[it, q * 2], gat[it, q * 2 + 1]
        acc[0] += jnp.dot(jnp.concatenate([v0, v1], axis=1), block(q), preferred_element_type=F32)
        ed = jnp.dot(jnp.concatenate([v0, v1], axis=0), low[...], preferred_element_type=F32)
        high = elb[:, 8:9, :]
        high = jnp.concatenate([high[0], high[1]], axis=1)
        acc[1] += jnp.where(high == q * 2, ed[:B], 0.0) + jnp.where(high == q * 2 + 1, ed[B:], 0.0)

    def coef(i):
        return jnp.concatenate([co[0, i], co[1, i]], axis=1)

    def reduce_src(it, tiles):
        lane_tile = coef(0) * acc[1] + coef(1) * acc[0]
        for half in range(2):
            ar_s[it, 6 * half:6 * half + 6] = lane_tile[:, 128 * half:128 * half + 128].reshape(6, 8, 128)

        def send(t, carry):
            owner = 2 * t + c

            @pl.when(owner != src)
            def _():
                remote(ar_s.at[it, t], ar_in.at[it, src], a1_send.at[it], a1_recv.at[it], (owner, rcv)).start()
            return carry

        lax.fori_loop(0, tiles, send, 0)
        mine = src - c
        is_owner = (lax.rem(mine + 2, 2) == 0) & (mine >= 0) & (mine < 2 * tiles)

        @pl.when(is_owner)
        def _():
            t = mine // 2
            ar_in[it, src] = ar_s[it, t]
            wait_recv(ar_in.at[it, pl.ds(0, N_SRC - 1)], a1_recv.at[it])
            ar_out[it, t] = jnp.sum(ar_in[it], axis=0)

            def spread(d, carry):
                remote(ar_out.at[it, t], ar_out.at[it, t], a2_send.at[it], a2_recv.at[it],
                       (lax.rem(src + d, N_SRC), rcv)).start()
                return carry

            lax.fori_loop(1, N_SRC, spread, 0)
            wait_recv(ar_out.at[it, pl.ds(0, tiles - 1)], a2_recv.at[it])
            wait_send(ar_s.at[it, pl.ds(0, tiles - 1)], a1_send.at[it])

        @pl.when(jnp.logical_not(is_owner))
        def _():
            wait_recv(ar_out.at[it, pl.ds(0, tiles)], a2_recv.at[it])
            wait_send(ar_s.at[it, pl.ds(0, tiles)], a1_send.at[it])

        return jnp.concatenate(
            [ar_out[it, 6 * half:6 * half + 6].reshape(B, 128) for half in range(2)], axis=1)

    def finish_src(it, tiles):
        mine = src - c
        is_owner = (lax.rem(mine + 2, 2) == 0) & (mine >= 0) & (mine < 2 * tiles)

        @pl.when(is_owner)
        def _():
            wait_send(ar_in.at[it, pl.ds(0, N_SRC - 1)], a2_send.at[it])

    def share_scalars(it, tile):
        tb[it, rcv] = tile

        def send(d, carry):
            remote(tb.at[it, rcv], tb.at[it, rcv], t_send.at[it], t_recv.at[it],
                   (src, lax.rem(rcv + d, N_RCV))).start()
            return carry

        lax.fori_loop(1, N_RCV, send, 0)

    def sum_scalars(it):
        wait_recv(tb.at[it, pl.ds(0, N_RCV - 1)], t_recv.at[it])
        return jnp.sum(tb[it], axis=0)

    def scatter_sources(it, jv, scalars=None):
        w = (coef(1) * jv).astype(BF16)
        lift = coef(0) * jv
        high = jnp.concatenate([elb[0, 8:9, :], elb[1, 8:9, :]], axis=1)

        def part(d):
            q = chip(d)
            both = dot_nt(w, block(q))
            sparse = jnp.concatenate(
                [jnp.where(high == q * 2, lift, 0.0), jnp.where(high == q * 2 + 1, lift, 0.0)], axis=0)
            spread = dot_nt(sparse.astype(BF16), low[...])
            return both[:, :L] + spread[:B], both[:, L:] + spread[B:]

        def send(slot, value, to, landing):
            rs_send[it, slot] = value.astype(BF16)
            remote(rs_send.at[it, slot], rs_in.at[it, landing], rs_ssem.at[it], rs_recv.at[it, landing],
                   at_chip(to, c)).start()

        def home(slot, value, d, h):
            rs_send[it, slot] = value.astype(BF16)
            landing = {1: 0, -1: 2, 2: 4, -2: 6}[d] + c
            remote(rs_send.at[it, slot], rs_fin.at[it, landing], rs_ssem.at[it], rf_recv.at[it, landing],
                   at_chip(d, h)).start()

        def came(landing):
            wait_recv(rs_in.at[it, landing], rs_recv.at[it, landing])
            return rs_in[it, landing].astype(F32)

        far = part(4)
        send(0, far[0], 2, 0)
        send(1, far[1], -2, 1)
        for k, d in enumerate((1, -1)):
            far = part(3 * d)
            send(2 + 2 * k, far[0], d, 2 + 2 * k)
            send(3 + 2 * k, far[1], d, 3 + 2 * k)
        for k, d in enumerate((1, -1)):
            near = part(d)
            home(6 + 2 * k, near[0], d, 0)
            home(7 + 2 * k, near[1], d, 1)
        if scalars is not None:
            share_scalars(it, scalars)
        up, down, mine = part(2), part(-2), part(0)
        own[it, 0] = mine[0]
        own[it, 1] = mine[1]
        remote(own.at[it, other], sib.at[it], sp_send.at[it], sp_recv.at[it], here).start()
        home(10, up[1] + came(3), 2, 1)
        home(11, down[0] + came(4), -2, 0)
        home(12, up[0] + came(2) + came(0), 2, 0)
        home(13, down[1] + came(5) + came(1), -2, 1)

    def sources_sum(it):
        wait_recv(sib.at[it], sp_recv.at[it])
        out = []
        for comp in range(2):
            total = jnp.where(c == comp, own[it, c], sib[it])
            for way in range(4):
                slot = way * 2 + comp
                wait_recv(rs_fin.at[it, slot], rf_recv.at[it, slot])
                total += rs_fin[it, slot].astype(F32)
            out.append(total)
        return out

    gather_start(0)
    co_share = remote(co_send, co.at[c], sib_send.at[0], sib_recv.at[0], here)
    co_share.start()
    el_share = remote(elb.at[c, pl.ds(0, 8)], elb.at[c, pl.ds(0, 8)], sib_send.at[1], sib_recv.at[1], here)
    el_share.start()
    for d in (0, 1, -1, 2, -2):
        share_k(d)
    acc[...] = jnp.zeros((2, B, 256), F32)
    wait_recv(elb.at[other, pl.ds(0, 8)], sib_recv.at[1])
    place = jnp.concatenate([elb[0, 0:1, :], elb[1, 0:1, :]], axis=1) - src * (NY * 2 * L)
    low[...] = jnp.where(
        lax.broadcasted_iota(jnp.int32, (L, 256), 0) == (place & (L - 1)), 1.0, 0.0).astype(BF16)
    high = place >> 8
    elb[0, 8:, :] = jnp.broadcast_to(high[:, :128], (8, 128))
    elb[1, 8:, :] = jnp.broadcast_to(high[:, 128:], (8, 128))
    k_copy.wait()

    relay(0)
    for d in (3, -3, 4):
        share_k(d)

    def add_all(it):
        arrived(it, 0, other)
        add_chip(it, 0)
        for d in (1, -1):
            arrived(it, d, 0)
            arrived(it, d, 1)
            add_chip(it, d)
        for d in (2, -2):
            add_chip(it, d)
        for d in (3, -3, 4):
            arrived(it, d, 0)
            arrived(it, d, 1)
            add_chip(it, d)

    add_all(0)
    wait_recv(co.at[other], sib_recv.at[0])
    jv = reduce_src(0, TILES - 1)
    j0[...] = jv
    gp_row = row_of(jv * jv)
    scatter_sources(0, jv)
    p0, p1 = sources_sum(0)

    stage(1, p0, p1)
    gather_start(1)
    p_ref[0] = p0
    p_ref[1] = p1
    pp_row = row_of(p0 * p0 + p1 * p1)
    share_scalars(0, jnp.concatenate(
        [gg_row, pp_row, gp_row * (1.0 / N_SRC), jnp.zeros((5, 128), F32)], axis=0))
    acc[...] = jnp.zeros((2, B, 256), F32)
    relay(1)
    add_all(1)
    ar_s[1, TILES - 1] = sum_scalars(0)
    jp = reduce_src(1, TILES)
    sums = ar_out[1, TILES - 1]
    gg, pp, gp = sums[0:1], sums[1:2], sums[2:3]
    alpha0 = gg / (0.5 * gg + gp)
    left = gp / (0.5 * gg + gp)
    rr = alpha0 * (alpha0 * pp - left * gp)
    beta = rr / gg
    scale = left + beta
    alpha0_c, left_c, scale_c = col_of(alpha0), col_of(left), col_of(scale)
    jv = scale_c * j0[...] - alpha0_c * jp
    scatter_sources(1, jv, jnp.broadcast_to(row_of(jv * jv), (8, 128)))
    jj = sum_scalars(1)[0:1]
    alpha1 = rr / (0.5 * rr * (1.0 + beta) + jj)
    alpha1_c = col_of(alpha1)
    base = []
    for comp in range(2):
        gv = g_ref[:, comp, :]
        pv = p_ref[comp]
        direction = scale_c * gv - alpha0_c * pv
        x_ref[:, comp, :] = alpha0_c * gv + alpha1_c * direction
        base.append(left_c * gv - alpha0_c * pv - alpha1_c * (0.5 * direction))
    x_out = pltpu.make_async_copy(x_ref, x_hbm, out_sem.at[0])
    x_out.start()
    q = sources_sum(1)
    for comp in range(2):
        r_ref[:, comp, :] = base[comp] - alpha1_c * q[comp]
    r_out = pltpu.make_async_copy(r_ref, r_hbm, out_sem.at[1])
    r_out.start()

    co_share.wait_send()
    el_share.wait_send()
    wait_send(kw.at[c], kp_send)
    for it in range(2):
        wait_send(gat.at[it, pl.ds(0, 15)], ag_send.at[it])
        wait_send(rs_send.at[it, pl.ds(0, 14)], rs_ssem.at[it])
        wait_send(own.at[it, 0], sp_send.at[it])
        wait_send(tb.at[it, pl.ds(0, N_RCV - 1)], t_send.at[it])
        finish_src(it, TILES - 1 + it)
    x_out.wait()
    r_out.wait()


def shards(stiffness, newton_rhs, traction, opening, state, elements):
    dma, vmem = pltpu.SemaphoreType.DMA, pltpu.VMEM
    out = jax.ShapeDtypeStruct((B, 2, L), F32)
    return pl.pallas_call(
        kernel,
        out_shape=(out, out),
        in_specs=[pl.BlockSpec(memory_space=pl.ANY)] * 6,
        out_specs=[pl.BlockSpec(memory_space=pl.ANY)] * 2,
        scratch_shapes=[
            vmem((B, 2, L), F32),
            vmem((B, 2, 128), F32),
            vmem((B, 128), F32),
            vmem((B, 128), jnp.int32),
            vmem((1, 128), jnp.int32),
            vmem((B, 2, L), F32),
            vmem((B, 2, L), F32),
            vmem((2, NY * 2 * L, 128), BF16),
            vmem((L, 256), BF16),
            vmem((2, 16, 128), jnp.int32),
            vmem((2, 2, B, 128), F32),
            vmem((2, B, 128), F32),
            vmem((2, 2, B, L), BF16),
            vmem((2, 16, B, L), BF16),
            vmem((2, B, 256), F32),
            vmem((B, 256), F32),
            vmem((2, TILES, 8, 128), F32),
            vmem((2, N_SRC, 8, 128), F32),
            vmem((2, TILES, 8, 128), F32),
            vmem((2, 16, B, L), BF16),
            vmem((2, 6, B, L), BF16),
            vmem((2, 8, B, L), BF16),
            vmem((2, 2, B, L), F32),
            vmem((2, B, L), F32),
            vmem((2, B, L), F32),
            vmem((2, N_RCV, 8, 128), F32),
            dma, dma((5,)), dma((2,)), dma((2,)), dma((2,)), dma, dma((NY,)),
            dma((2,)), dma((2, 16)), dma((2,)), dma((2, 6)), dma((2, 8)),
            dma((2,)), dma((2,)), dma((2,)), dma((2,)), dma((2,)), dma((2,)), dma((2,)), dma((2,)),
        ],
        compiler_params=pltpu.CompilerParams(
            collective_id=0, has_side_effects=True, vmem_limit_bytes=60 * 1024 * 1024),
        cost_estimate=pl.CostEstimate(flops=8 * B * 4096 * 512, bytes_accessed=4 << 20, transcendentals=0),
    )(stiffness, newton_rhs, traction, opening, state, elements.reshape(1, 128))


def solution(mesh):
    placed = (
        P(None, "src", "rcv"),
        P(None, None, ("src", "rcv")),
        P(None, None, "rcv"),
        P(None, "rcv"),
        P(None, "rcv"),
        P("rcv"),
    )
    return jax.shard_map(
        shards,
        mesh=mesh,
        in_specs=placed,
        out_specs=(P(None, None, ("src", "rcv")), P(None, None, ("src", "rcv"))),
        check_vma=False,
    )
```

time: 823 us -> 85.6 us (0.10)
  blocking collectives: 568 us -> 0 us
  waiting for transfers between devices: 160 us -> 0 us
  Pallas kernels: 0 us -> 81.7 us
  local copies, waits for them, and re-layouts: 40.7 us -> 3.08 us
  other arithmetic: 34 us -> 0 us
  between operations: 14.2 us -> 0.64 us
    psum x5 -> x0, blocking collectives: 526 us -> none  [the longest x2 232 us: shards(): jv = lax.psum(coef_a * ed_sum + coef_b * kd_sum, 'src')]
    reduce_scatter x2 -> x0, waiting for transfers between devices: 160 us -> none  [shards(): summed = lax.psum_scatter(term, 'rcv', scatter_dimension=2, tiled=True)]
    pallas_call x0 -> x1, Pallas kernels: none -> 81.7 us  [shards(): pl.pallas_call(kernel, out_shape=(out, out), in_specs=[pl.BlockSpec(memor...]
    all_gather x2 -> x0, blocking collectives: 41.6 us -> none  [shards(): piece = lax.all_gather(apply_vb, 'rcv', axis=2, tiled=True)]
    scatter-add x2 -> x0, other arithmetic: 27.7 us -> none  [shards(): term = term.at[:, :, drop_index].add(lifted, mode='drop')]
    scatter-add x2 -> x0, local copies, waits for them, and re-layouts: 12.5 us -> none  [shards(): term = term.at[:, :, drop_index].add(lifted, mode='drop')]
    transpose x2 -> x0, local copies, waits for them, and re-layouts: 12.1 us -> none  [shards(): jnp.einsum('bcr,csr->bcs', weighted, stiffness, preferred_element_type=jn...]
  transfers between devices with their start and end apart: 2 -> 0, of which waited for: 2 -> 0; matrix products, arithmetic and copies ran while one was open for 0% -> 0% of each run, Pallas kernels for 0% -> 0%
where the time goes in v1:
time: 85.6 us; the launch traced here: 85.4 us
  Pallas kernels  81.7 us (95%)
  local copies, waits for them, and re-layouts  3.08 us (4%)
    pallas_call x1, Pallas kernels, shards(): pl.pallas_call(kernel, out_shape=(out, out), in_specs=[pl.BlockSpec(memor...  81.7 us
    unnamed x2, local copies, waits for them, and re-layouts  3.08 us

profile of v1, /device:TPU:1, one launch (start us, length us, event | category | flops | bytes accessed | tf_op | source)
XLA Modules:
  0.0 85.4 jit_solution(6706356878066419167)
XLA Ops:
  0.6 81.7 %shard_map.77 = (f32[48,2,256]{2,1,0:T(2,128)}, f32[48,2,256]{2,1,0:T(2,128)}) custom-call(bf16[2,4096,128]{2,1,0:T(8,128)(2,1)} %k_hbm.1, f32[48,2,256]{2,1,0:T(2,128)} %g_hbm.1, f32[48,2,128]{2,1,0:T(2,128)} %tr_hbm.1, f32[48,128]{1,0:T(8,128)} %op_hbm.1, s32[48,128]{1,0:T(8,128)} %st_hbm.1, s32[1,128]{1,0:T(1,128)} %bitcast.1), custom_call_target="tpu_custom_call" | custom-call | flops 805306368 | bytes 4194304 | tf_op jit(solution)/shard_map/pallas_call | solution.py:386
  82.3 1.5 %copy.10 = f32[48,2,256]{2,1,0:T(2,128)} copy(f32[48,2,256]{2,1,0:T(2,128)} %get-tuple-element.4) | data formatting | bytes 196608
  83.9 1.5 %copy.11 = f32[48,2,256]{2,1,0:T(2,128)} copy(f32[48,2,256]{2,1,0:T(2,128)} %get-tuple-element.5) | data formatting | bytes 196608

commit v2 on v1

v2 whole, which is shorter than its diff:
```python
import jax
import jax.numpy as jnp
from jax import lax
from jax.experimental import pallas as pl
from jax.experimental.pallas import tpu as pltpu
from jax.sharding import PartitionSpec as P

MESH = pl.DeviceIdType.MESH
F32 = jnp.float32
BF16 = jnp.bfloat16
B = 48
L = 256
NY = 8
N_RCV = 16
N_SRC = 32
TILES = 6


def dot_nt(a, b):
    return lax.dot_general(a, b, (((1,), (1,)), ((), ())), preferred_element_type=F32)


def kernel(k_hbm, g_hbm, tr_hbm, op_hbm, st_hbm, el_hbm, x_hbm, r_hbm,
           g_ref, tr_ref, op_ref, st_ref, el_ref, x_ref, r_ref,
           kw, low, elb, co, co_send, sb, gat, acc, j0, ar_s, ar_in, ar_out, sc_s, sc_in, sc_out,
           rs_send, rs_in, rs_fin, own, pown, sib, tb,
           k_sem, in_sem, out_sem, sib_send, sib_recv, kp_send, kp_recv, ag_send, ag_recv, rs_ssem, rs_recv, rf_recv,
           sp_send, sp_recv, a1_send, a1_recv, a2_send, a2_recv,
           s1_send, s1_recv, s2_send, s2_recv, t_send, t_recv):
    src = lax.axis_index("src")
    rcv = lax.axis_index("rcv")
    y = rcv // 2
    c = lax.rem(rcv, 2)
    other = 1 - c

    def chip(d):
        return lax.rem(y + d + NY, NY)

    def at_chip(d, core):
        return (src, chip(d) * 2 + core)

    def remote(s, d, ss, rs, dev):
        return pltpu.make_async_remote_copy(
            src_ref=s, dst_ref=d, send_sem=ss, recv_sem=rs, device_id=dev, device_id_type=MESH)

    here = (src, y * 2 + other)

    def wait_recv(ref, sem):
        remote(ref, ref, sem, sem, here).wait_recv()

    def wait_send(ref, sem):
        remote(ref, ref, sem, sem, here).wait_send()

    loads = [
        pltpu.make_async_copy(a, b, in_sem.at[i])
        for i, (a, b) in enumerate((
            (g_hbm, g_ref), (tr_hbm, tr_ref), (op_hbm, op_ref), (st_hbm, st_ref), (el_hbm, el_ref)))
    ]
    for load in loads:
        load.start()

    barrier = pltpu.get_barrier_semaphore()

    def greet(dev):
        pl.semaphore_signal(barrier, inc=1, device_id=dev, device_id_type=MESH)

    def greet_rcv(d, carry):
        greet((src, lax.rem(rcv + d, N_RCV)))
        return carry

    def greet_src(d, carry):
        greet((lax.rem(src + d, N_SRC), rcv))
        return carry

    lax.fori_loop(1, N_RCV, greet_rcv, 0)
    lax.fori_loop(1, N_SRC, greet_src, 0)

    k_copy = pltpu.make_async_copy(k_hbm.at[c], kw.at[c], k_sem)
    k_copy.start()

    lane = lax.broadcasted_iota(jnp.int32, (B, 128), 1)
    case = lax.broadcasted_iota(jnp.int32, (B, 128), 0)
    diag = lane == case

    def row_of(v):
        col = jnp.sum(v, axis=1, keepdims=True)
        return jnp.sum(jnp.where(diag, col, 0.0), axis=0, keepdims=True)

    def col_of(row):
        return jnp.sum(jnp.where(diag, row, 0.0), axis=1, keepdims=True)

    loads[0].wait()
    g0, g1 = g_ref[:, 0, :], g_ref[:, 1, :]
    b0, b1 = g0.astype(BF16), g1.astype(BF16)
    sb[0] = b0
    sb[1] = b1
    gat[0, rcv] = jnp.where(c == 0, b0, b1)
    gg_row = row_of(g0 * g0 + g1 * g1)

    pl.semaphore_wait(barrier, N_RCV + N_SRC - 2)

    for ways in ((2, -2), (1, -1)):
        for comp in range(2):
            for d in ways:
                remote(sb.at[comp], gat.at[0, rcv], ag_send.at[0], ag_recv.at[0, rcv], at_chip(d, comp)).start()
    remote(sb.at[other], gat.at[0, rcv], ag_send.at[0], ag_recv.at[0, rcv], here).start()

    def share_k(d):
        q = chip(d)
        rows = pl.ds(pl.multiple_of(q * (2 * L), 2 * L), 2 * L)
        remote(k_hbm.at[other, rows], kw.at[c, rows], kp_send, kp_recv.at[q], here).start()

    def arrived(it, d, h):
        slot = chip(d) * 2 + h
        wait_recv(gat.at[it, slot], ag_recv.at[it, slot])

    def relay(it):
        for h in range(2):
            for d in (1, -1):
                arrived(it, -2 * d, h)
                slot = chip(-2 * d) * 2 + h
                part = gat.at[it, slot]
                if (d == 1) == (h == 0):
                    remote(part, part, ag_send.at[it], ag_recv.at[it, slot], at_chip(2 * d, c)).start()
                remote(part, part, ag_send.at[it], ag_recv.at[it, slot], at_chip(d, c)).start()

    def block(q):
        rows = pl.ds(pl.multiple_of(q * (2 * L), 2 * L), 2 * L)
        return jnp.concatenate([kw[0, rows, :], kw[1, rows, :]], axis=1)

    def add_chip(it, d):
        q = chip(d)
        if it == 0:
            rows = pl.ds(pl.multiple_of(q * (2 * L), 2 * L), 2 * L)
            wait_recv(kw.at[other, rows], kp_recv.at[q])
        v0, v1 = gat[it, q * 2], gat[it, q * 2 + 1]
        acc[0] += jnp.dot(jnp.concatenate([v0, v1], axis=1), block(q), preferred_element_type=F32)
        ed = jnp.dot(jnp.concatenate([v0, v1], axis=0), low[...], preferred_element_type=F32)
        high = elb[:, 8:9, :]
        high = jnp.concatenate([high[0], high[1]], axis=1)
        acc[1] += jnp.where(high == q * 2, ed[:B], 0.0) + jnp.where(high == q * 2 + 1, ed[B:], 0.0)

    def coef(i):
        return jnp.concatenate([co[0, i], co[1, i]], axis=1)

    def others(send):
        def one(d, carry):
            send((lax.rem(src + d, N_SRC), rcv))
            return carry

        lax.fori_loop(1, N_SRC, one, 0)

    tile = (src - 2 * c + 5) // 5 - 1
    sums_tile = (lax.rem(src - 2 * c + 5, 5) == 0) & (tile >= 0) & (tile < TILES)
    sums_scalars = src == 30 + c

    def reduce_src(it):
        part = (coef(0) * acc[1] + coef(1) * acc[0]).astype(BF16)
        for half in range(2):
            ar_s[it, 3 * half:3 * half + 3] = part[:, 128 * half:128 * half + 128].reshape(3, 16, 128)

        def send(t, carry):
            owner = 5 * t + 2 * c

            @pl.when(owner != src)
            def _():
                remote(ar_s.at[it, t], ar_in.at[it, src], a1_send.at[it], a1_recv.at[it], (owner, rcv)).start()
            return carry

        lax.fori_loop(0, TILES, send, 0)
        if it == 1:
            sc_s[...] = sum_scalars(0)

            @pl.when(jnp.logical_not(sums_scalars))
            def _():
                remote(sc_s, sc_in.at[src], s1_send, s1_recv, (30 + c, rcv)).start()

            @pl.when(sums_scalars)
            def _():
                sc_in[src] = sc_s[...]
                wait_recv(sc_in.at[pl.ds(0, N_SRC - 1)], s1_recv)
                sc_out[...] = jnp.sum(sc_in[...], axis=0)
                others(lambda dev: remote(sc_out, sc_out, s2_send, s2_recv, dev).start())

        @pl.when(sums_tile)
        def _():
            ar_in[it, src] = ar_s[it, tile]
            wait_recv(ar_in.at[it, pl.ds(0, N_SRC - 1)], a1_recv.at[it])
            ar_out[it, tile] = jnp.sum(ar_in[it].astype(F32), axis=0).astype(BF16)
            part = ar_out.at[it, tile]
            others(lambda dev: remote(part, part, a2_send.at[it], a2_recv.at[it], dev).start())
            wait_recv(ar_out.at[it, pl.ds(0, TILES - 1)], a2_recv.at[it])

        @pl.when(jnp.logical_not(sums_tile))
        def _():
            wait_recv(ar_out.at[it, pl.ds(0, TILES)], a2_recv.at[it])

        if it == 1:
            pl.when(jnp.logical_not(sums_scalars))(lambda: wait_recv(sc_out, s2_recv))
        return jnp.concatenate(
            [ar_out[it, 3 * half:3 * half + 3].reshape(B, 128) for half in range(2)], axis=1).astype(F32)

    def finish_src(it):
        @pl.when(sums_tile)
        def _():
            wait_send(ar_in.at[it, pl.ds(0, N_SRC - 1)], a2_send.at[it])
            wait_send(ar_s.at[it, pl.ds(0, TILES - 1)], a1_send.at[it])

        @pl.when(jnp.logical_not(sums_tile))
        def _():
            wait_send(ar_s.at[it, pl.ds(0, TILES)], a1_send.at[it])

        if it == 1:
            pl.when(sums_scalars)(lambda: wait_send(sc_in.at[pl.ds(0, N_SRC - 1)], s2_send))
            pl.when(jnp.logical_not(sums_scalars))(lambda: wait_send(sc_s, s1_send))

    def share_scalars(it, tile):
        tb[it, rcv] = tile

        def send(d, carry):
            remote(tb.at[it, rcv], tb.at[it, rcv], t_send.at[it], t_recv.at[it],
                   (src, lax.rem(rcv + d, N_RCV))).start()
            return carry

        lax.fori_loop(1, N_RCV, send, 0)

    def sum_scalars(it):
        wait_recv(tb.at[it, pl.ds(0, N_RCV - 1)], t_recv.at[it])
        return jnp.sum(tb[it], axis=0)

    def scatter_sources(it, jv, scalars=None):
        w = (coef(1) * jv).astype(BF16)
        lift = coef(0) * jv
        high = jnp.concatenate([elb[0, 8:9, :], elb[1, 8:9, :]], axis=1)

        def part(d):
            q = chip(d)
            both = dot_nt(w, block(q))
            sparse = jnp.concatenate(
                [jnp.where(high == q * 2, lift, 0.0), jnp.where(high == q * 2 + 1, lift, 0.0)], axis=0)
            spread = dot_nt(sparse.astype(BF16), low[...])
            return both[:, :L] + spread[:B], both[:, L:] + spread[B:]

        def send(slot, value, to, landing):
            rs_send[it, slot] = value.astype(BF16)
            remote(rs_send.at[it, slot], rs_in.at[it, landing], rs_ssem.at[it], rs_recv.at[it, landing],
                   at_chip(to, c)).start()

        def home(slot, value, d, h):
            rs_send[it, slot] = value.astype(BF16)
            landing = {1: 0, -1: 2, 2: 4, -2: 6}[d] + (h if it == 0 else c)
            remote(rs_send.at[it, slot], rs_fin.at[it, landing], rs_ssem.at[it], rf_recv.at[it, landing],
                   at_chip(d, c if it == 0 else h)).start()

        def came(landing):
            wait_recv(rs_in.at[it, landing], rs_recv.at[it, landing])
            return rs_in[it, landing].astype(F32)

        for k, d in enumerate((1, -1)):
            far = part(3 * d)
            send(2 + 2 * k, far[0], d, 2 + 2 * k)
            send(3 + 2 * k, far[1], d, 3 + 2 * k)
        far = part(4)
        send(0, far[0], 2, 0)
        send(1, far[1], -2, 1)
        for k, d in enumerate((1, -1)):
            near = part(d)
            home(6 + 2 * k, near[0], d, 0)
            home(7 + 2 * k, near[1], d, 1)
        if scalars is not None:
            share_scalars(it, scalars())
        up, down, mine = part(2), part(-2), part(0)
        own[it, 0] = mine[0]
        own[it, 1] = mine[1]
        if it == 1:
            remote(own.at[it, other], sib.at[it], sp_send.at[it], sp_recv.at[it], here).start()
        home(10, up[1] + came(3), 2, 1)
        home(11, down[0] + came(4), -2, 0)
        home(12, up[0] + came(2) + came(0), 2, 0)
        home(13, down[1] + came(5) + came(1), -2, 1)

    def arrivals(it, i):
        total = 0.0
        for way in range(4):
            slot = way * 2 + i
            wait_recv(rs_fin.at[it, slot], rf_recv.at[it, slot])
            total += rs_fin[it, slot].astype(F32)
        return total

    for load in loads[1:]:
        load.wait()
    tau, press = tr_ref[:, 0, :], tr_ref[:, 1, :]
    opening, state = op_ref[...], st_ref[...]
    radius = jnp.sqrt(opening * opening + press * press + 0.5)
    a_n = 1.0 - opening / radius
    b_n = 1.0 - press / radius
    ratio = jnp.abs(tau) / (1.0 + 0.6 * jnp.abs(press))
    a_s = jnp.where(state == 0, 1.0, jnp.where(state == 1, ratio, 0.0))
    b_s = jnp.where(state == 0, ratio, 1.0)
    co[c, 0] = jnp.where(c == 0, a_s, a_n)
    co[c, 1] = jnp.where(c == 0, b_s, b_n)
    co_send[0] = jnp.where(c == 0, a_n, a_s)
    co_send[1] = jnp.where(c == 0, b_n, b_s)
    elb[c, :8, :] = jnp.broadcast_to(el_ref[...], (8, 128))
    co_share = remote(co_send, co.at[c], sib_send.at[0], sib_recv.at[0], here)
    co_share.start()
    el_share = remote(elb.at[c, pl.ds(0, 8)], elb.at[c, pl.ds(0, 8)], sib_send.at[1], sib_recv.at[1], here)
    el_share.start()
    for d in (0, 1, -1, 2, -2):
        share_k(d)
    acc[...] = jnp.zeros((2, B, 256), F32)
    wait_recv(elb.at[other, pl.ds(0, 8)], sib_recv.at[1])
    for d in (3, -3, 4):
        share_k(d)
    place = jnp.concatenate([elb[0, 0:1, :], elb[1, 0:1, :]], axis=1) - src * (NY * 2 * L)
    low[...] = jnp.where(
        lax.broadcasted_iota(jnp.int32, (L, 256), 0) == (place & (L - 1)), 1.0, 0.0).astype(BF16)
    high = place >> 8
    elb[0, 8:, :] = jnp.broadcast_to(high[:, :128], (8, 128))
    elb[1, 8:, :] = jnp.broadcast_to(high[:, 128:], (8, 128))
    k_copy.wait()

    relay(0)

    def add_all(it):
        if it == 0:
            arrived(it, 0, other)
        add_chip(it, 0)
        for d in (1, -1):
            arrived(it, d, 0)
            arrived(it, d, 1)
            add_chip(it, d)
        for d in (2, -2):
            add_chip(it, d)
        for d in (3, -3, 4):
            arrived(it, d, 0)
            arrived(it, d, 1)
            add_chip(it, d)

    add_all(0)
    wait_recv(co.at[other], sib_recv.at[0])
    jv = reduce_src(0)
    j0[...] = jv
    scatter_sources(0, jv)
    gp_row = row_of(jv * jv)

    pp = 0.0
    for h in range(2):
        p = own[0, h] + arrivals(0, h)
        pown[h] = p
        pp += p * p
        part = gat.at[1, y * 2 + h]
        part[...] = p.astype(BF16)
        for d in (2, -2):
            remote(part, part, ag_send.at[1], ag_recv.at[1, y * 2 + h], at_chip(d, c)).start()
    for h in range(2):
        part = gat.at[1, y * 2 + h]
        for d in (1, -1):
            remote(part, part, ag_send.at[1], ag_recv.at[1, y * 2 + h], at_chip(d, c)).start()
    remote(pown.at[other], sib.at[0], sp_send.at[0], sp_recv.at[0], here).start()
    pp_row = row_of(pp)
    share_scalars(0, jnp.concatenate(
        [gg_row, pp_row, gp_row * (1.0 / N_SRC), jnp.zeros((5, 128), F32)], axis=0))
    acc[...] = jnp.zeros((2, B, 256), F32)
    relay(1)
    add_all(1)
    jp = reduce_src(1)
    sums = sc_out[...]
    gg, pp, gp = sums[0:1], sums[1:2], sums[2:3]
    alpha0 = gg / (0.5 * gg + gp)
    left = gp / (0.5 * gg + gp)
    rr = alpha0 * (alpha0 * pp - left * gp)
    beta = rr / gg
    scale = left + beta
    alpha0_c, left_c, scale_c = col_of(alpha0), col_of(left), col_of(scale)
    jv = scale_c * j0[...] - alpha0_c * jp
    scatter_sources(1, jv, lambda: jnp.broadcast_to(row_of(jv * jv), (8, 128)))
    jj = sum_scalars(1)[0:1]
    alpha1 = rr / (0.5 * rr * (1.0 + beta) + jj)
    alpha1_c = col_of(alpha1)
    wait_recv(sib.at[0], sp_recv.at[0])
    base = []
    for comp in range(2):
        gv = g_ref[:, comp, :]
        pv = jnp.where(c == comp, pown[c], sib[0])
        direction = scale_c * gv - alpha0_c * pv
        x_ref[:, comp, :] = alpha0_c * gv + alpha1_c * direction
        base.append(left_c * gv - alpha0_c * pv - alpha1_c * (0.5 * direction))
    x_out = pltpu.make_async_copy(x_ref, x_hbm, out_sem.at[0])
    x_out.start()
    wait_recv(sib.at[1], sp_recv.at[1])
    for comp in range(2):
        q = jnp.where(c == comp, own[1, c], sib[1]) + arrivals(1, comp)
        r_ref[:, comp, :] = base[comp] - alpha1_c * q
    r_out = pltpu.make_async_copy(r_ref, r_hbm, out_sem.at[1])
    r_out.start()

    co_share.wait_send()
    el_share.wait_send()
    wait_send(kw.at[c], kp_send)
    for it in range(2):
        wait_send(gat.at[it, pl.ds(0, 15 - it)], ag_send.at[it])
        wait_send(rs_send.at[it, pl.ds(0, 14)], rs_ssem.at[it])
        wait_send(own.at[it, 0], sp_send.at[it])
        wait_send(tb.at[it, pl.ds(0, N_RCV - 1)], t_send.at[it])
        finish_src(it)
    x_out.wait()
    r_out.wait()


def hand_on(x_in, r_in, x_out, r_out, sem):
    copies = [pltpu.make_async_copy(x_in, x_out, sem.at[0]), pltpu.make_async_copy(r_in, r_out, sem.at[1])]
    for copy in copies:
        copy.start()
    for copy in copies:
        copy.wait()


def shards(stiffness, newton_rhs, traction, opening, state, elements):
    dma, vmem = pltpu.SemaphoreType.DMA, pltpu.VMEM
    out = jax.ShapeDtypeStruct((B, 2, L), F32)
    x, r = pl.pallas_call(
        kernel,
        out_shape=(out, out),
        in_specs=[pl.BlockSpec(memory_space=pl.ANY)] * 6,
        out_specs=[pl.BlockSpec(memory_space=pl.ANY)] * 2,
        scratch_shapes=[
            vmem((B, 2, L), F32),
            vmem((B, 2, 128), F32),
            vmem((B, 128), F32),
            vmem((B, 128), jnp.int32),
            vmem((1, 128), jnp.int32),
            vmem((B, 2, L), F32),
            vmem((B, 2, L), F32),
            vmem((2, NY * 2 * L, 128), BF16),
            vmem((L, 256), BF16),
            vmem((2, 16, 128), jnp.int32),
            vmem((2, 2, B, 128), F32),
            vmem((2, B, 128), F32),
            vmem((2, B, L), BF16),
            vmem((2, 16, B, L), BF16),
            vmem((2, B, 256), F32),
            vmem((B, 256), F32),
            vmem((2, TILES, 16, 128), BF16),
            vmem((2, N_SRC, 16, 128), BF16),
            vmem((2, TILES, 16, 128), BF16),
            vmem((8, 128), F32),
            vmem((N_SRC, 8, 128), F32),
            vmem((8, 128), F32),
            vmem((2, 16, B, L), BF16),
            vmem((2, 6, B, L), BF16),
            vmem((2, 8, B, L), BF16),
            vmem((2, 2, B, L), F32),
            vmem((2, B, L), F32),
            vmem((2, B, L), F32),
            vmem((2, N_RCV, 8, 128), F32),
            dma, dma((5,)), dma((2,)), dma((2,)), dma((2,)), dma, dma((NY,)),
            dma((2,)), dma((2, 16)), dma((2,)), dma((2, 6)), dma((2, 8)),
            dma((2,)), dma((2,)), dma((2,)), dma((2,)), dma((2,)), dma((2,)), dma, dma, dma, dma, dma((2,)), dma((2,)),
        ],
        compiler_params=pltpu.CompilerParams(
            collective_id=0, has_side_effects=True, vmem_limit_bytes=60 * 1024 * 1024),
        cost_estimate=pl.CostEstimate(flops=8 * B * 4096 * 512, bytes_accessed=4 << 20, transcendentals=0),
    )(stiffness, newton_rhs, traction, opening, state, elements.reshape(1, 128))
    anywhere = [pl.BlockSpec(memory_space=pl.ANY)] * 2
    return pl.pallas_call(
        hand_on, out_shape=(out, out), in_specs=anywhere, out_specs=anywhere, scratch_shapes=[dma((2,))],
        compiler_params=pltpu.CompilerParams(vmem_limit_bytes=60 * 1024 * 1024))(x, r)


def solution(mesh):
    placed = (
        P(None, "src", "rcv"),
        P(None, None, ("src", "rcv")),
        P(None, None, "rcv"),
        P(None, "rcv"),
        P(None, "rcv"),
        P("rcv"),
    )
    return jax.shard_map(
        shards,
        mesh=mesh,
        in_specs=placed,
        out_specs=(P(None, None, ("src", "rcv")), P(None, None, ("src", "rcv"))),
        check_vma=False,
    )
```

time: 85.6 us -> 84.8 us (level)
  local copies, waits for them, and re-layouts: 3.08 us -> 0 us
  Pallas kernels: 81.7 us -> 84 us
    pallas_call x0 -> x1, Pallas kernels: none -> 7.08 us  [shards(): pl.pallas_call(hand_on, out_shape=(out, out), in_specs=anywhere, out_spec...]
    pallas_call x1, Pallas kernels: 81.7 us -> 77 us  [shards(): pl.pallas_call(kernel, out_shape=(out, out), in_specs=[pl.BlockSpec(memor...]
    unnamed x2 -> x0, local copies, waits for them, and re-layouts: 3.08 us -> none
where the time goes in v2:
time: 84.8 us; the launch traced here: 84.7 us
  Pallas kernels  84 us (99%)
    pallas_call x1, Pallas kernels, shards(): pl.pallas_call(kernel, out_shape=(out, out), in_specs=[pl.BlockSpec(memor...  77 us
    pallas_call x1, Pallas kernels, shards(): pl.pallas_call(hand_on, out_shape=(out, out), in_specs=anywhere, out_spec...  7.08 us

profile of v2, /device:TPU:1, one launch (start us, length us, event | category | flops | bytes accessed | tf_op | source)
XLA Modules:
  0.0 84.7 jit_solution(600826047150141740)
XLA Ops:
  0.6 77.0 %shard_map.77 = (f32[48,2,256]{2,1,0:T(2,128)}, f32[48,2,256]{2,1,0:T(2,128)}) custom-call(bf16[2,4096,128]{2,1,0:T(8,128)(2,1)} %k_hbm.1, f32[48,2,256]{2,1,0:T(2,128)} %g_hbm.1, f32[48,2,128]{2,1,0:T(2,128)} %tr_hbm.1, f32[48,128]{1,0:T(8,128)} %op_hbm.1, s32[48,128]{1,0:T(8,128)} %st_hbm.1, s32[1,128]{1,0:T(1,128)} %bitcast.1), custom_call_target="tpu_custom_call" | custom-call | flops 805306368 | bytes 4194304 | tf_op jit(solution)/shard_map/pallas_call | solution.py:422
  77.6 7.1 %shard_map.78 = (f32[48,2,256]{2,1,0:T(2,128)}, f32[48,2,256]{2,1,0:T(2,128)}) custom-call(f32[48,2,256]{2,1,0:T(2,128)} %get-tuple-element.4.x_in, f32[48,2,256]{2,1,0:T(2,128)} %get-tuple-element.5.r_in), custom_call_target="tpu_custom_call" | custom-call | tf_op jit(solution)/shard_map/pallas_call | solution.py:466

commit v3 on v2

--- a/solution.py
+++ b/solution.py
@@ -22,7 +22,7 @@
 
 def kernel(k_hbm, g_hbm, tr_hbm, op_hbm, st_hbm, el_hbm, x_hbm, r_hbm,
            g_ref, tr_ref, op_ref, st_ref, el_ref, x_ref, r_ref,
-           kw, low, elb, co, co_send, sb, gat, acc, j0, ar_s, ar_in, ar_out, sc_s, sc_in, sc_out,
+           kw, k_own, low, elb, co, co_send, sb, gat, acc, j0, ar_s, ar_in, ar_out, sc_s, sc_in, sc_out,
            rs_send, rs_in, rs_fin, own, pown, sib, tb,
            k_sem, in_sem, out_sem, sib_send, sib_recv, kp_send, kp_recv, ag_send, ag_recv, rs_ssem, rs_recv, rf_recv,
            sp_send, sp_recv, a1_send, a1_recv, a2_send, a2_recv,
@@ -75,7 +75,9 @@
     lax.fori_loop(1, N_RCV, greet_rcv, 0)
     lax.fori_loop(1, N_SRC, greet_src, 0)
 
-    k_copy = pltpu.make_async_copy(k_hbm.at[c], kw.at[c], k_sem)
+    k_away = pltpu.make_async_copy(k_hbm.at[other], k_own, k_sem.at[1])
+    k_away.start()
+    k_copy = pltpu.make_async_copy(k_hbm.at[c], kw.at[c], k_sem.at[0])
     k_copy.start()
 
     lane = lax.broadcasted_iota(jnp.int32, (B, 128), 1)
@@ -108,7 +110,7 @@
     def share_k(d):
         q = chip(d)
         rows = pl.ds(pl.multiple_of(q * (2 * L), 2 * L), 2 * L)
-        remote(k_hbm.at[other, rows], kw.at[c, rows], kp_send, kp_recv.at[q], here).start()
+        remote(k_own.at[rows], kw.at[c, rows], kp_send, kp_recv.at[q], here).start()
 
     def arrived(it, d, h):
         slot = chip(d) * 2 + h
@@ -306,6 +308,7 @@
     co_share.start()
     el_share = remote(elb.at[c, pl.ds(0, 8)], elb.at[c, pl.ds(0, 8)], sib_send.at[1], sib_recv.at[1], here)
     el_share.start()
+    k_away.wait()
     for d in (0, 1, -1, 2, -2):
         share_k(d)
     acc[...] = jnp.zeros((2, B, 256), F32)
@@ -408,18 +411,10 @@
     r_out.wait()
 
 
-def hand_on(x_in, r_in, x_out, r_out, sem):
-    copies = [pltpu.make_async_copy(x_in, x_out, sem.at[0]), pltpu.make_async_copy(r_in, r_out, sem.at[1])]
-    for copy in copies:
-        copy.start()
-    for copy in copies:
-        copy.wait()
-
-
 def shards(stiffness, newton_rhs, traction, opening, state, elements):
     dma, vmem = pltpu.SemaphoreType.DMA, pltpu.VMEM
     out = jax.ShapeDtypeStruct((B, 2, L), F32)
-    x, r = pl.pallas_call(
+    return pl.pallas_call(
         kernel,
         out_shape=(out, out),
         in_specs=[pl.BlockSpec(memory_space=pl.ANY)] * 6,
@@ -433,6 +428,7 @@
             vmem((B, 2, L), F32),
             vmem((B, 2, L), F32),
             vmem((2, NY * 2 * L, 128), BF16),
+            vmem((NY * 2 * L, 128), BF16),
             vmem((L, 256), BF16),
             vmem((2, 16, 128), jnp.int32),
             vmem((2, 2, B, 128), F32),
@@ -454,7 +450,7 @@
             vmem((2, B, L), F32),
             vmem((2, B, L), F32),
             vmem((2, N_RCV, 8, 128), F32),
-            dma, dma((5,)), dma((2,)), dma((2,)), dma((2,)), dma, dma((NY,)),
+            dma((2,)), dma((5,)), dma((2,)), dma((2,)), dma((2,)), dma, dma((NY,)),
             dma((2,)), dma((2, 16)), dma((2,)), dma((2, 6)), dma((2, 8)),
             dma((2,)), dma((2,)), dma((2,)), dma((2,)), dma((2,)), dma((2,)), dma, dma, dma, dma, dma((2,)), dma((2,)),
         ],
@@ -462,10 +458,6 @@
             collective_id=0, has_side_effects=True, vmem_limit_bytes=60 * 1024 * 1024),
         cost_estimate=pl.CostEstimate(flops=8 * B * 4096 * 512, bytes_accessed=4 << 20, transcendentals=0),
     )(stiffness, newton_rhs, traction, opening, state, elements.reshape(1, 128))
-    anywhere = [pl.BlockSpec(memory_space=pl.ANY)] * 2
-    return pl.pallas_call(
-        hand_on, out_shape=(out, out), in_specs=anywhere, out_specs=anywhere, scratch_shapes=[dma((2,))],
-        compiler_params=pltpu.CompilerParams(vmem_limit_bytes=60 * 1024 * 1024))(x, r)
 
 
 def solution(mesh):

time: 84.8 us -> 80.9 us (0.954)
  Pallas kernels: 84 us -> 77 us
  local copies, waits for them, and re-layouts: 0 us -> 3.08 us
    pallas_call x1 -> x0, Pallas kernels: 7.08 us -> none  [shards(): pl.pallas_call(hand_on, out_shape=(out, out), in_specs=anywhere, out_spec...]
    unnamed x0 -> x2, local copies, waits for them, and re-layouts: none -> 3.08 us
where the time goes in v3:
time: 80.9 us; the launch traced here: 80.7 us
  Pallas kernels  77 us (95%)
  local copies, waits for them, and re-layouts  3.08 us (4%)
    pallas_call x1, Pallas kernels, shards(): pl.pallas_call(kernel, out_shape=(out, out), in_specs=[pl.BlockSpec(memor...  77 us
    unnamed x2, local copies, waits for them, and re-layouts  3.08 us

profile of v3, /device:TPU:1, one launch (start us, length us, event | category | flops | bytes accessed | tf_op | source)
XLA Modules:
  0.0 80.7 jit_solution(13629075148485414854)
XLA Ops:
  0.6 77.0 %shard_map.77 = (f32[48,2,256]{2,1,0:T(2,128)}, f32[48,2,256]{2,1,0:T(2,128)}) custom-call(bf16[2,4096,128]{2,1,0:T(8,128)(2,1)} %k_hbm.1, f32[48,2,256]{2,1,0:T(2,128)} %g_hbm.1, f32[48,2,128]{2,1,0:T(2,128)} %tr_hbm.1, f32[48,128]{1,0:T(8,128)} %op_hbm.1, s32[48,128]{1,0:T(8,128)} %st_hbm.1, s32[1,128]{1,0:T(1,128)} %bitcast.1), custom_call_target="tpu_custom_call" | custom-call | flops 805306368 | bytes 4194304 | tf_op jit(solution)/shard_map/pallas_call | solution.py:417
  77.6 1.5 %copy.10 = f32[48,2,256]{2,1,0:T(2,128)} copy(f32[48,2,256]{2,1,0:T(2,128)} %get-tuple-element.4) | data formatting | bytes 196608
  79.1 1.5 %copy.11 = f32[48,2,256]{2,1,0:T(2,128)} copy(f32[48,2,256]{2,1,0:T(2,128)} %get-tuple-element.5) | data formatting | bytes 196608

commit v4 on v3

--- a/solution.py
+++ b/solution.py
@@ -14,17 +14,18 @@
 N_RCV = 16
 N_SRC = 32
 TILES = 6
+ORDER = (0, 1, -1, 2, -2, 3, -3, 4)
 
 
 def dot_nt(a, b):
     return lax.dot_general(a, b, (((1,), (1,)), ((), ())), preferred_element_type=F32)
 
 
-def kernel(k_hbm, g_hbm, tr_hbm, op_hbm, st_hbm, el_hbm, x_hbm, r_hbm,
-           g_ref, tr_ref, op_ref, st_ref, el_ref, x_ref, r_ref,
+def kernel(k_hbm, g_hbm, tr_hbm, op_hbm, st_hbm, el_hbm, x_ref, r_ref,
+           g_ref, tr_ref, op_ref, st_ref, el_ref,
            kw, k_own, low, elb, co, co_send, sb, gat, acc, j0, ar_s, ar_in, ar_out, sc_s, sc_in, sc_out,
            rs_send, rs_in, rs_fin, own, pown, sib, tb,
-           k_sem, in_sem, out_sem, sib_send, sib_recv, kp_send, kp_recv, ag_send, ag_recv, rs_ssem, rs_recv, rf_recv,
+           k_sem, ka_sem, g_sem, in_sem, sib_send, sib_recv, kp_send, kp_recv, ag_send, ag_recv, rs_ssem, rs_recv, rf_recv,
            sp_send, sp_recv, a1_send, a1_recv, a2_send, a2_recv,
            s1_send, s1_recv, s2_send, s2_recv, t_send, t_recv):
     src = lax.axis_index("src")
@@ -51,10 +52,14 @@
     def wait_send(ref, sem):
         remote(ref, ref, sem, sem, here).wait_send()
 
+    g_loads = [
+        pltpu.make_async_copy(g_hbm.at[pl.ds(8 * i, 8)], g_ref.at[pl.ds(8 * i, 8)], g_sem.at[i]) for i in range(B // 8)]
+    for load in g_loads:
+        load.start()
     loads = [
         pltpu.make_async_copy(a, b, in_sem.at[i])
         for i, (a, b) in enumerate((
-            (g_hbm, g_ref), (tr_hbm, tr_ref), (op_hbm, op_ref), (st_hbm, st_ref), (el_hbm, el_ref)))
+            (tr_hbm, tr_ref), (op_hbm, op_ref), (st_hbm, st_ref), (el_hbm, el_ref)))
     ]
     for load in loads:
         load.start()
@@ -75,10 +80,18 @@
     lax.fori_loop(1, N_RCV, greet_rcv, 0)
     lax.fori_loop(1, N_SRC, greet_src, 0)
 
-    k_away = pltpu.make_async_copy(k_hbm.at[other], k_own, k_sem.at[1])
-    k_away.start()
-    k_copy = pltpu.make_async_copy(k_hbm.at[c], kw.at[c], k_sem.at[0])
-    k_copy.start()
+    def k_rows(d):
+        return pl.ds(pl.multiple_of(chip(d) * (2 * L), 2 * L), 2 * L)
+
+    def k_away(d):
+        return pltpu.make_async_copy(k_hbm.at[other, k_rows(d)], k_own.at[k_rows(d)], ka_sem.at[chip(d)])
+
+    def k_copy(d):
+        return pltpu.make_async_copy(k_hbm.at[c, k_rows(d)], kw.at[c, k_rows(d)], k_sem.at[chip(d)])
+
+    for d in ORDER:
+        k_away(d).start()
+        k_copy(d).start()
 
     lane = lax.broadcasted_iota(jnp.int32, (B, 128), 1)
     case = lax.broadcasted_iota(jnp.int32, (B, 128), 0)
@@ -91,7 +104,8 @@
     def col_of(row):
         return jnp.sum(jnp.where(diag, row, 0.0), axis=1, keepdims=True)
 
-    loads[0].wait()
+    for load in g_loads:
+        load.wait()
     g0, g1 = g_ref[:, 0, :], g_ref[:, 1, :]
     b0, b1 = g0.astype(BF16), g1.astype(BF16)
     sb[0] = b0
@@ -101,16 +115,16 @@
 
     pl.semaphore_wait(barrier, N_RCV + N_SRC - 2)
 
-    for ways in ((2, -2), (1, -1)):
-        for comp in range(2):
-            for d in ways:
-                remote(sb.at[comp], gat.at[0, rcv], ag_send.at[0], ag_recv.at[0, rcv], at_chip(d, comp)).start()
+    def first_sends(comp):
+        for d in (2, -2, 1, -1):
+            remote(sb.at[comp], gat.at[0, rcv], ag_send.at[0], ag_recv.at[0, rcv], at_chip(d, comp)).start()
+
+    first_sends(0)
     remote(sb.at[other], gat.at[0, rcv], ag_send.at[0], ag_recv.at[0, rcv], here).start()
 
     def share_k(d):
-        q = chip(d)
-        rows = pl.ds(pl.multiple_of(q * (2 * L), 2 * L), 2 * L)
-        remote(k_own.at[rows], kw.at[c, rows], kp_send, kp_recv.at[q], here).start()
+        k_away(d).wait()
+        remote(k_own.at[k_rows(d)], kw.at[c, k_rows(d)], kp_send, kp_recv.at[chip(d)], here).start()
 
     def arrived(it, d, h):
         slot = chip(d) * 2 + h
@@ -133,8 +147,8 @@
     def add_chip(it, d):
         q = chip(d)
         if it == 0:
-            rows = pl.ds(pl.multiple_of(q * (2 * L), 2 * L), 2 * L)
-            wait_recv(kw.at[other, rows], kp_recv.at[q])
+            k_copy(d).wait()
+            wait_recv(kw.at[other, k_rows(d)], kp_recv.at[q])
         v0, v1 = gat[it, q * 2], gat[it, q * 2 + 1]
         acc[0] += jnp.dot(jnp.concatenate([v0, v1], axis=1), block(q), preferred_element_type=F32)
         ed = jnp.dot(jnp.concatenate([v0, v1], axis=0), low[...], preferred_element_type=F32)
@@ -289,7 +303,7 @@
             total += rs_fin[it, slot].astype(F32)
         return total
 
-    for load in loads[1:]:
+    for load in loads:
         load.wait()
     tau, press = tr_ref[:, 0, :], tr_ref[:, 1, :]
     opening, state = op_ref[...], st_ref[...]
@@ -308,12 +322,12 @@
     co_share.start()
     el_share = remote(elb.at[c, pl.ds(0, 8)], elb.at[c, pl.ds(0, 8)], sib_send.at[1], sib_recv.at[1], here)
     el_share.start()
-    k_away.wait()
-    for d in (0, 1, -1, 2, -2):
+    for d in ORDER[:5]:
         share_k(d)
+    first_sends(1)
     acc[...] = jnp.zeros((2, B, 256), F32)
     wait_recv(elb.at[other, pl.ds(0, 8)], sib_recv.at[1])
-    for d in (3, -3, 4):
+    for d in ORDER[5:]:
         share_k(d)
     place = jnp.concatenate([elb[0, 0:1, :], elb[1, 0:1, :]], axis=1) - src * (NY * 2 * L)
     low[...] = jnp.where(
@@ -321,7 +335,6 @@
     high = place >> 8
     elb[0, 8:, :] = jnp.broadcast_to(high[:, :128], (8, 128))
     elb[1, 8:, :] = jnp.broadcast_to(high[:, 128:], (8, 128))
-    k_copy.wait()
 
     relay(0)
 
@@ -389,14 +402,10 @@
         direction = scale_c * gv - alpha0_c * pv
         x_ref[:, comp, :] = alpha0_c * gv + alpha1_c * direction
         base.append(left_c * gv - alpha0_c * pv - alpha1_c * (0.5 * direction))
-    x_out = pltpu.make_async_copy(x_ref, x_hbm, out_sem.at[0])
-    x_out.start()
     wait_recv(sib.at[1], sp_recv.at[1])
     for comp in range(2):
         q = jnp.where(c == comp, own[1, c], sib[1]) + arrivals(1, comp)
         r_ref[:, comp, :] = base[comp] - alpha1_c * q
-    r_out = pltpu.make_async_copy(r_ref, r_hbm, out_sem.at[1])
-    r_out.start()
 
     co_share.wait_send()
     el_share.wait_send()
@@ -407,8 +416,6 @@
         wait_send(own.at[it, 0], sp_send.at[it])
         wait_send(tb.at[it, pl.ds(0, N_RCV - 1)], t_send.at[it])
         finish_src(it)
-    x_out.wait()
-    r_out.wait()
 
 
 def shards(stiffness, newton_rhs, traction, opening, state, elements):
@@ -418,15 +425,13 @@
         kernel,
         out_shape=(out, out),
         in_specs=[pl.BlockSpec(memory_space=pl.ANY)] * 6,
-        out_specs=[pl.BlockSpec(memory_space=pl.ANY)] * 2,
+        out_specs=[pl.BlockSpec(memory_space=pltpu.VMEM)] * 2,
         scratch_shapes=[
             vmem((B, 2, L), F32),
             vmem((B, 2, 128), F32),
             vmem((B, 128), F32),
             vmem((B, 128), jnp.int32),
             vmem((1, 128), jnp.int32),
-            vmem((B, 2, L), F32),
-            vmem((B, 2, L), F32),
             vmem((2, NY * 2 * L, 128), BF16),
             vmem((NY * 2 * L, 128), BF16),
             vmem((L, 256), BF16),
@@ -450,14 +455,15 @@
             vmem((2, B, L), F32),
             vmem((2, B, L), F32),
             vmem((2, N_RCV, 8, 128), F32),
-            dma((2,)), dma((5,)), dma((2,)), dma((2,)), dma((2,)), dma, dma((NY,)),
+            dma((NY,)), dma((NY,)), dma((B // 8,)), dma((4,)), dma((2,)), dma((2,)), dma, dma((NY,)),
             dma((2,)), dma((2, 16)), dma((2,)), dma((2, 6)), dma((2, 8)),
             dma((2,)), dma((2,)), dma((2,)), dma((2,)), dma((2,)), dma((2,)), dma, dma, dma, dma, dma((2,)), dma((2,)),
         ],
         compiler_params=pltpu.CompilerParams(
-            collective_id=0, has_side_effects=True, vmem_limit_bytes=60 * 1024 * 1024),
+            collective_id=0, has_side_effects=True, vmem_limit_bytes=24 * 1024 * 1024),
         cost_estimate=pl.CostEstimate(flops=8 * B * 4096 * 512, bytes_accessed=4 << 20, transcendentals=0),
-    )(stiffness, newton_rhs, traction, opening, state, elements.reshape(1, 128))
+    )(*(pltpu.with_memory_space_constraint(a, pltpu.HBM) for a in (
+        stiffness, newton_rhs, traction, opening, state, elements.reshape(1, 128))))
 
 
 def solution(mesh):

time: 80.9 us -> 78.3 us (0.968)
  local copies, waits for them, and re-layouts: 3.08 us -> 1.28 us
    unnamed x2, local copies, waits for them, and re-layouts: 3.08 us -> 1.28 us
where the time goes in v4:
time: 78.3 us; the launch traced here: 78.1 us
  Pallas kernels  76.2 us (97%)
  local copies, waits for them, and re-layouts  1.28 us (2%)
    pallas_call x1, Pallas kernels, shards(): pl.pallas_call(kernel, out_shape=(out, out), in_specs=[pl.BlockSpec(memor...  76.2 us

profile of v4, /device:TPU:1, one launch (start us, length us, event | category | flops | bytes accessed | tf_op | source)
XLA Modules:
  0.0 78.1 jit_solution(15833240349833899637)
XLA Ops:
  0.6 76.2 %shard_map.77 = (f32[48,2,256]{2,1,0:T(2,128)S(1)}, f32[48,2,256]{2,1,0:T(2,128)S(1)}) custom-call(bf16[2,4096,128]{2,1,0:T(8,128)(2,1)} %k_hbm.1, f32[48,2,256]{2,1,0:T(2,128)} %g_hbm.1, f32[48,2,128]{2,1,0:T(2,128)} %tr_hbm.1, f32[48,128]{1,0:T(8,128)} %op_hbm.1, s32[48,128]{1,0:T(8,128)} %st_hbm.1, s32[1,128]{1,0:T(1,128)} %bitcast.1), custom_call_target="tpu_custom_call" | custom-call | flops 805306368 | bytes 4194304 | tf_op jit(solution)/shard_map/pallas_call | solution.py:424
  76.9 0.6 copy.10
  77.5 0.6 copy.11

commit v5 on v4

--- a/solution.py
+++ b/solution.py
@@ -14,7 +14,10 @@
 N_RCV = 16
 N_SRC = 32
 TILES = 6
-ORDER = (0, 1, -1, 2, -2, 3, -3, 4)
+
+
+def away(i):
+    return (i + 1) // 2 * (2 * (i % 2) - 1)
 
 
 def dot_nt(a, b):
@@ -24,7 +27,7 @@
 def kernel(k_hbm, g_hbm, tr_hbm, op_hbm, st_hbm, el_hbm, x_ref, r_ref,
            g_ref, tr_ref, op_ref, st_ref, el_ref,
            kw, k_own, low, elb, co, co_send, sb, gat, acc, j0, ar_s, ar_in, ar_out, sc_s, sc_in, sc_out,
-           rs_send, rs_in, rs_fin, own, pown, sib, tb,
+           rs_send, rs_in, rs_fin, fresh, pown, sib, tb, rows,
            k_sem, ka_sem, g_sem, in_sem, sib_send, sib_recv, kp_send, kp_recv, ag_send, ag_recv, rs_ssem, rs_recv, rf_recv,
            sp_send, sp_recv, a1_send, a1_recv, a2_send, a2_recv,
            s1_send, s1_recv, s2_send, s2_recv, t_send, t_recv):
@@ -89,9 +92,12 @@
     def k_copy(d):
         return pltpu.make_async_copy(k_hbm.at[c, k_rows(d)], kw.at[c, k_rows(d)], k_sem.at[chip(d)])
 
-    for d in ORDER:
-        k_away(d).start()
-        k_copy(d).start()
+    def k_start(i, carry):
+        k_away(away(i)).start()
+        k_copy(away(i)).start()
+        return carry
+
+    lax.fori_loop(0, NY, k_start, 0)
 
     lane = lax.broadcasted_iota(jnp.int32, (B, 128), 1)
     case = lax.broadcasted_iota(jnp.int32, (B, 128), 0)
@@ -111,7 +117,7 @@
     sb[0] = b0
     sb[1] = b1
     gat[0, rcv] = jnp.where(c == 0, b0, b1)
-    gg_row = row_of(g0 * g0 + g1 * g1)
+    rows[0:1, :] = row_of(g0 * g0 + g1 * g1)
 
     pl.semaphore_wait(barrier, N_RCV + N_SRC - 2)
 
@@ -122,9 +128,11 @@
     first_sends(0)
     remote(sb.at[other], gat.at[0, rcv], ag_send.at[0], ag_recv.at[0, rcv], here).start()
 
-    def share_k(d):
+    def share_k(i, carry):
+        d = away(i)
         k_away(d).wait()
         remote(k_own.at[k_rows(d)], kw.at[c, k_rows(d)], kp_send, kp_recv.at[chip(d)], here).start()
+        return carry
 
     def arrived(it, d, h):
         slot = chip(d) * 2 + h
@@ -144,17 +152,35 @@
         rows = pl.ds(pl.multiple_of(q * (2 * L), 2 * L), 2 * L)
         return jnp.concatenate([kw[0, rows, :], kw[1, rows, :]], axis=1)
 
-    def add_chip(it, d):
-        q = chip(d)
-        if it == 0:
-            k_copy(d).wait()
-            wait_recv(kw.at[other, k_rows(d)], kp_recv.at[q])
-        v0, v1 = gat[it, q * 2], gat[it, q * 2 + 1]
-        acc[0] += jnp.dot(jnp.concatenate([v0, v1], axis=1), block(q), preferred_element_type=F32)
-        ed = jnp.dot(jnp.concatenate([v0, v1], axis=0), low[...], preferred_element_type=F32)
-        high = elb[:, 8:9, :]
-        high = jnp.concatenate([high[0], high[1]], axis=1)
-        acc[1] += jnp.where(high == q * 2, ed[:B], 0.0) + jnp.where(high == q * 2 + 1, ed[B:], 0.0)
+    def high_bits():
+        return jnp.concatenate([elb[0, 8:9, :], elb[1, 8:9, :]], axis=1)
+
+    def add_chips(it):
+        acc[...] = jnp.zeros((2, B, 256), F32)
+
+        def add_chip(i, carry):
+            d = away(i)
+            q = chip(d)
+
+            @pl.when(it == 0)
+            def _():
+                k_copy(d).wait()
+                wait_recv(kw.at[other, k_rows(d)], kp_recv.at[q])
+                pl.when(i == 0)(lambda: arrived(0, 0, other))
+
+            @pl.when((i >= 1) & ((i < 3) | (i > 4)))
+            def _():
+                arrived(it, d, 0)
+                arrived(it, d, 1)
+
+            v0, v1 = gat[it, q * 2], gat[it, q * 2 + 1]
+            acc[0] += jnp.dot(jnp.concatenate([v0, v1], axis=1), block(q), preferred_element_type=F32)
+            ed = jnp.dot(jnp.concatenate([v0, v1], axis=0), low[...], preferred_element_type=F32)
+            high = high_bits()
+            acc[1] += jnp.where(high == q * 2, ed[:B], 0.0) + jnp.where(high == q * 2 + 1, ed[B:], 0.0)
+            return carry
+
+        lax.fori_loop(0, NY, add_chip, 0)
 
     def coef(i):
         return jnp.concatenate([co[0, i], co[1, i]], axis=1)
@@ -184,7 +210,9 @@
             return carry
 
         lax.fori_loop(0, TILES, send, 0)
-        if it == 1:
+
+        @pl.when(it == 1)
+        def _():
             sc_s[...] = sum_scalars(0)
 
             @pl.when(jnp.logical_not(sums_scalars))
@@ -211,8 +239,7 @@
         def _():
             wait_recv(ar_out.at[it, pl.ds(0, TILES)], a2_recv.at[it])
 
-        if it == 1:
-            pl.when(jnp.logical_not(sums_scalars))(lambda: wait_recv(sc_out, s2_recv))
+        pl.when((it == 1) & jnp.logical_not(sums_scalars))(lambda: wait_recv(sc_out, s2_recv))
         return jnp.concatenate(
             [ar_out[it, 3 * half:3 * half + 3].reshape(B, 128) for half in range(2)], axis=1).astype(F32)
 
@@ -244,56 +271,69 @@
         wait_recv(tb.at[it, pl.ds(0, N_RCV - 1)], t_recv.at[it])
         return jnp.sum(tb[it], axis=0)
 
-    def scatter_sources(it, jv, scalars=None):
+    def scatter_sources(it, jv):
         w = (coef(1) * jv).astype(BF16)
         lift = coef(0) * jv
-        high = jnp.concatenate([elb[0, 8:9, :], elb[1, 8:9, :]], axis=1)
-
-        def part(d):
-            q = chip(d)
+
+        def home(slot, d, h):
+            landing = {1: 0, -1: 2, 2: 4, -2: 6}[d] + h + it * (c - h)
+            remote(rs_send.at[it, slot], rs_fin.at[it, landing], rs_ssem.at[it], rf_recv.at[it, landing],
+                   at_chip(d, c + it * (h - c))).start()
+
+        def came(landing):
+            wait_recv(rs_in.at[it, landing], rs_recv.at[it, landing])
+            return rs_in[it, landing].astype(F32)
+
+        def part(i, carry):
+            q = chip(away(lax.rem(i + 5, NY)))
+            high = high_bits()
             both = dot_nt(w, block(q))
             sparse = jnp.concatenate(
                 [jnp.where(high == q * 2, lift, 0.0), jnp.where(high == q * 2 + 1, lift, 0.0)], axis=0)
             spread = dot_nt(sparse.astype(BF16), low[...])
-            return both[:, :L] + spread[:B], both[:, L:] + spread[B:]
-
-        def send(slot, value, to, landing):
-            rs_send[it, slot] = value.astype(BF16)
-            remote(rs_send.at[it, slot], rs_in.at[it, landing], rs_ssem.at[it], rs_recv.at[it, landing],
-                   at_chip(to, c)).start()
-
-        def home(slot, value, d, h):
-            rs_send[it, slot] = value.astype(BF16)
-            landing = {1: 0, -1: 2, 2: 4, -2: 6}[d] + (h if it == 0 else c)
-            remote(rs_send.at[it, slot], rs_fin.at[it, landing], rs_ssem.at[it], rf_recv.at[it, landing],
-                   at_chip(d, c if it == 0 else h)).start()
-
-        def came(landing):
-            wait_recv(rs_in.at[it, landing], rs_recv.at[it, landing])
-            return rs_in[it, landing].astype(F32)
-
-        for k, d in enumerate((1, -1)):
-            far = part(3 * d)
-            send(2 + 2 * k, far[0], d, 2 + 2 * k)
-            send(3 + 2 * k, far[1], d, 3 + 2 * k)
-        far = part(4)
-        send(0, far[0], 2, 0)
-        send(1, far[1], -2, 1)
-        for k, d in enumerate((1, -1)):
-            near = part(d)
-            home(6 + 2 * k, near[0], d, 0)
-            home(7 + 2 * k, near[1], d, 1)
-        if scalars is not None:
-            share_scalars(it, scalars())
-        up, down, mine = part(2), part(-2), part(0)
-        own[it, 0] = mine[0]
-        own[it, 1] = mine[1]
-        if it == 1:
-            remote(own.at[it, other], sib.at[it], sp_send.at[it], sp_recv.at[it], here).start()
-        home(10, up[1] + came(3), 2, 1)
-        home(11, down[0] + came(4), -2, 0)
-        home(12, up[0] + came(2) + came(0), 2, 0)
-        home(13, down[1] + came(5) + came(1), -2, 1)
+            for h in range(2):
+                value = both[:, h * L:h * L + L] + spread[h * B:h * B + B]
+                fresh[i, h] = value
+                rs_send[it, 2 * i + h] = value.astype(BF16)
+
+            def onward(h, to, landing):
+                remote(rs_send.at[it, 2 * i + h], rs_in.at[it, landing], rs_ssem.at[it], rs_recv.at[it, landing],
+                       at_chip(to, c)).start()
+
+            for at, d in ((0, 1), (1, -1)):
+                @pl.when(i == at)
+                def _():
+                    onward(0, d, 2 + 2 * at)
+                    onward(1, d, 3 + 2 * at)
+
+                @pl.when(i == 4 + at)
+                def _():
+                    home(8 + 2 * at, d, 0)
+                    home(9 + 2 * at, d, 1)
+
+            @pl.when(i == 2)
+            def _():
+                onward(0, 2, 0)
+                onward(1, -2, 1)
+
+            @pl.when((i == 3) & (it == 1))
+            def _():
+                remote(fresh.at[3, other], sib.at[1], sp_send.at[1], sp_recv.at[1], here).start()
+            return carry
+
+        lax.fori_loop(0, NY, part, 0)
+
+        @pl.when(it == 1)
+        def _():
+            share_scalars(1, jnp.broadcast_to(row_of(jv * jv), (8, 128)))
+
+        for d, h, relays in ((2, 1, (3,)), (-2, 0, (4,)), (2, 0, (2, 0)), (-2, 1, (5, 1))):
+            at = 6 if d == 2 else 7
+            value = fresh[at, h]
+            for landing in relays:
+                value += came(landing)
+            rs_send[it, 2 * at + h] = value.astype(BF16)
+            home(2 * at + h, d, h)
 
     def arrivals(it, i):
         total = 0.0
@@ -322,13 +362,10 @@
     co_share.start()
     el_share = remote(elb.at[c, pl.ds(0, 8)], elb.at[c, pl.ds(0, 8)], sib_send.at[1], sib_recv.at[1], here)
     el_share.start()
-    for d in ORDER[:5]:
-        share_k(d)
+    lax.fori_loop(0, 5, share_k, 0)
     first_sends(1)
-    acc[...] = jnp.zeros((2, B, 256), F32)
     wait_recv(elb.at[other, pl.ds(0, 8)], sib_recv.at[1])
-    for d in ORDER[5:]:
-        share_k(d)
+    lax.fori_loop(5, NY, share_k, 0)
     place = jnp.concatenate([elb[0, 0:1, :], elb[1, 0:1, :]], axis=1) - src * (NY * 2 * L)
     low[...] = jnp.where(
         lax.broadcasted_iota(jnp.int32, (L, 256), 0) == (place & (L - 1)), 1.0, 0.0).astype(BF16)
@@ -336,64 +373,51 @@
     elb[0, 8:, :] = jnp.broadcast_to(high[:, :128], (8, 128))
     elb[1, 8:, :] = jnp.broadcast_to(high[:, 128:], (8, 128))
 
-    relay(0)
-
-    def add_all(it):
-        if it == 0:
-            arrived(it, 0, other)
-        add_chip(it, 0)
-        for d in (1, -1):
-            arrived(it, d, 0)
-            arrived(it, d, 1)
-            add_chip(it, d)
-        for d in (2, -2):
-            add_chip(it, d)
-        for d in (3, -3, 4):
-            arrived(it, d, 0)
-            arrived(it, d, 1)
-            add_chip(it, d)
-
-    add_all(0)
-    wait_recv(co.at[other], sib_recv.at[0])
-    jv = reduce_src(0)
-    j0[...] = jv
-    scatter_sources(0, jv)
-    gp_row = row_of(jv * jv)
-
-    pp = 0.0
-    for h in range(2):
-        p = own[0, h] + arrivals(0, h)
-        pown[h] = p
-        pp += p * p
-        part = gat.at[1, y * 2 + h]
-        part[...] = p.astype(BF16)
-        for d in (2, -2):
-            remote(part, part, ag_send.at[1], ag_recv.at[1, y * 2 + h], at_chip(d, c)).start()
-    for h in range(2):
-        part = gat.at[1, y * 2 + h]
-        for d in (1, -1):
-            remote(part, part, ag_send.at[1], ag_recv.at[1, y * 2 + h], at_chip(d, c)).start()
-    remote(pown.at[other], sib.at[0], sp_send.at[0], sp_recv.at[0], here).start()
-    pp_row = row_of(pp)
-    share_scalars(0, jnp.concatenate(
-        [gg_row, pp_row, gp_row * (1.0 / N_SRC), jnp.zeros((5, 128), F32)], axis=0))
-    acc[...] = jnp.zeros((2, B, 256), F32)
-    relay(1)
-    add_all(1)
-    jp = reduce_src(1)
-    sums = sc_out[...]
-    gg, pp, gp = sums[0:1], sums[1:2], sums[2:3]
-    alpha0 = gg / (0.5 * gg + gp)
-    left = gp / (0.5 * gg + gp)
-    rr = alpha0 * (alpha0 * pp - left * gp)
-    beta = rr / gg
-    scale = left + beta
-    alpha0_c, left_c, scale_c = col_of(alpha0), col_of(left), col_of(scale)
-    jv = scale_c * j0[...] - alpha0_c * jp
-    scatter_sources(1, jv, lambda: jnp.broadcast_to(row_of(jv * jv), (8, 128)))
+    j0[...] = jnp.zeros((B, 256), F32)
+    sc_out[...] = jnp.zeros((8, 128), F32)
+
+    def scalars():
+        gg, pp, gp = sc_out[0:1, :], sc_out[1:2, :], sc_out[2:3, :]
+        alpha0 = gg / (0.5 * gg + gp)
+        left = gp / (0.5 * gg + gp)
+        rr = alpha0 * (alpha0 * pp - left * gp)
+        return alpha0, left, rr, rr / gg
+
+    def apply(it, carry):
+        relay(it)
+        add_chips(it)
+        pl.when(it == 0)(lambda: wait_recv(co.at[other], sib_recv.at[0]))
+        image = reduce_src(it)
+        alpha0, left, rr, beta = scalars()
+        jv = jnp.where(it == 0, image, col_of(left + beta) * j0[...] - col_of(alpha0) * image)
+        j0[...] = jv
+        scatter_sources(it, jv)
+
+        @pl.when(it == 0)
+        def _():
+            pp = 0.0
+            for h in range(2):
+                p = fresh[3, h] + arrivals(0, h)
+                pown[h] = p
+                pp += p * p
+                part = gat.at[1, y * 2 + h]
+                part[...] = p.astype(BF16)
+                for d in (2, -2):
+                    remote(part, part, ag_send.at[1], ag_recv.at[1, y * 2 + h], at_chip(d, c)).start()
+            for h in range(2):
+                part = gat.at[1, y * 2 + h]
+                for d in (1, -1):
+                    remote(part, part, ag_send.at[1], ag_recv.at[1, y * 2 + h], at_chip(d, c)).start()
+            remote(pown.at[other], sib.at[0], sp_send.at[0], sp_recv.at[0], here).start()
+            share_scalars(0, jnp.concatenate(
+                [rows[0:1, :], row_of(pp), row_of(jv * jv) * (1.0 / N_SRC), jnp.zeros((5, 128), F32)], axis=0))
+        return carry
+
+    lax.fori_loop(0, 2, apply, 0)
+    alpha0, left, rr, beta = scalars()
+    alpha0_c, left_c, scale_c = col_of(alpha0), col_of(left), col_of(left + beta)
     jj = sum_scalars(1)[0:1]
-    alpha1 = rr / (0.5 * rr * (1.0 + beta) + jj)
-    alpha1_c = col_of(alpha1)
+    alpha1_c = col_of(rr / (0.5 * rr * (1.0 + beta) + jj))
     wait_recv(sib.at[0], sp_recv.at[0])
     base = []
     for comp in range(2):
@@ -404,7 +428,7 @@
         base.append(left_c * gv - alpha0_c * pv - alpha1_c * (0.5 * direction))
     wait_recv(sib.at[1], sp_recv.at[1])
     for comp in range(2):
-        q = jnp.where(c == comp, own[1, c], sib[1]) + arrivals(1, comp)
+        q = jnp.where(c == comp, fresh[3, c], sib[1]) + arrivals(1, comp)
         r_ref[:, comp, :] = base[comp] - alpha1_c * q
 
     co_share.wait_send()
@@ -413,7 +437,7 @@
     for it in range(2):
         wait_send(gat.at[it, pl.ds(0, 15 - it)], ag_send.at[it])
         wait_send(rs_send.at[it, pl.ds(0, 14)], rs_ssem.at[it])
-        wait_send(own.at[it, 0], sp_send.at[it])
+        wait_send(sib.at[it], sp_send.at[it])
         wait_send(tb.at[it, pl.ds(0, N_RCV - 1)], t_send.at[it])
         finish_src(it)
 
@@ -451,10 +475,11 @@
             vmem((2, 16, B, L), BF16),
             vmem((2, 6, B, L), BF16),
             vmem((2, 8, B, L), BF16),
-            vmem((2, 2, B, L), F32),
+            vmem((NY, 2, B, L), F32),
             vmem((2, B, L), F32),
             vmem((2, B, L), F32),
             vmem((2, N_RCV, 8, 128), F32),
+            vmem((8, 128), F32),
             dma((NY,)), dma((NY,)), dma((B // 8,)), dma((4,)), dma((2,)), dma((2,)), dma, dma((NY,)),
             dma((2,)), dma((2, 16)), dma((2,)), dma((2, 6)), dma((2, 8)),
             dma((2,)), dma((2,)), dma((2,)), dma((2,)), dma((2,)), dma((2,)), dma, dma, dma, dma, dma((2,)), dma((2,)),

time: 78.3 us -> 78.8 us (level)
  no operation moved by 1% of the time
where the time goes in v5:
time: 78.8 us; the launch traced here: 78.6 us
  Pallas kernels  76.7 us (97%)
  local copies, waits for them, and re-layouts  1.28 us (2%)
    pallas_call x1, Pallas kernels, shards(): pl.pallas_call(kernel, out_shape=(out, out), in_specs=[pl.BlockSpec(memor...  76.7 us

profile of v5, /device:TPU:1, one launch (start us, length us, event | category | flops | bytes accessed | tf_op | source)
XLA Modules:
  0.0 78.6 jit_solution(8715986146327382997)
XLA Ops:
  0.6 76.7 %shard_map.77 = (f32[48,2,256]{2,1,0:T(2,128)S(1)}, f32[48,2,256]{2,1,0:T(2,128)S(1)}) custom-call(bf16[2,4096,128]{2,1,0:T(8,128)(2,1)} %k_hbm.1, f32[48,2,256]{2,1,0:T(2,128)} %g_hbm.1, f32[48,2,128]{2,1,0:T(2,128)} %tr_hbm.1, f32[48,128]{1,0:T(8,128)} %op_hbm.1, s32[48,128]{1,0:T(8,128)} %st_hbm.1, s32[1,128]{1,0:T(1,128)} %bitcast.1), custom_call_target="tpu_custom_call" | custom-call | flops 805306368 | bytes 4194304 | tf_op jit(solution)/shard_map/pallas_call | solution.py:448
  77.3 0.6 copy.10
  78.0 0.6 copy.11

commit v6 on v4

--- a/solution.py
+++ b/solution.py
@@ -24,7 +24,7 @@
 def kernel(k_hbm, g_hbm, tr_hbm, op_hbm, st_hbm, el_hbm, x_ref, r_ref,
            g_ref, tr_ref, op_ref, st_ref, el_ref,
            kw, k_own, low, elb, co, co_send, sb, gat, acc, j0, ar_s, ar_in, ar_out, sc_s, sc_in, sc_out,
-           rs_send, rs_in, rs_fin, own, pown, sib, tb,
+           rs_send, rs_in, rs_fin, own, pown, sib, tb0, tb1,
            k_sem, ka_sem, g_sem, in_sem, sib_send, sib_recv, kp_send, kp_recv, ag_send, ag_recv, rs_ssem, rs_recv, rf_recv,
            sp_send, sp_recv, a1_send, a1_recv, a2_send, a2_recv,
            s1_send, s1_recv, s2_send, s2_recv, t_send, t_recv):
@@ -119,8 +119,11 @@
         for d in (2, -2, 1, -1):
             remote(sb.at[comp], gat.at[0, rcv], ag_send.at[0], ag_recv.at[0, rcv], at_chip(d, comp)).start()
 
+        @pl.when(c != comp)
+        def _():
+            remote(sb.at[comp], gat.at[0, rcv], ag_send.at[0], ag_recv.at[0, rcv], here).start()
+
     first_sends(0)
-    remote(sb.at[other], gat.at[0, rcv], ag_send.at[0], ag_recv.at[0, rcv], here).start()
 
     def share_k(d):
         k_away(d).wait()
@@ -230,19 +233,20 @@
             pl.when(sums_scalars)(lambda: wait_send(sc_in.at[pl.ds(0, N_SRC - 1)], s2_send))
             pl.when(jnp.logical_not(sums_scalars))(lambda: wait_send(sc_s, s1_send))
 
-    def share_scalars(it, tile):
-        tb[it, rcv] = tile
+    def share_scalars(it, row):
+        tb = (tb0, tb1)[it]
+        tb[rcv] = row
 
         def send(d, carry):
-            remote(tb.at[it, rcv], tb.at[it, rcv], t_send.at[it], t_recv.at[it],
-                   (src, lax.rem(rcv + d, N_RCV))).start()
+            remote(tb.at[rcv], tb.at[rcv], t_send.at[it], t_recv.at[it], (src, lax.rem(rcv + d, N_RCV))).start()
             return carry
 
         lax.fori_loop(1, N_RCV, send, 0)
 
     def sum_scalars(it):
-        wait_recv(tb.at[it, pl.ds(0, N_RCV - 1)], t_recv.at[it])
-        return jnp.sum(tb[it], axis=0)
+        tb = (tb0, tb1)[it]
+        wait_recv(tb.at[pl.ds(0, N_RCV - 1)], t_recv.at[it])
+        return jnp.sum(tb[...], axis=0)
 
     def scatter_sources(it, jv, scalars=None):
         w = (coef(1) * jv).astype(BF16)
@@ -324,7 +328,6 @@
     el_share.start()
     for d in ORDER[:5]:
         share_k(d)
-    first_sends(1)
     acc[...] = jnp.zeros((2, B, 256), F32)
     wait_recv(elb.at[other, pl.ds(0, 8)], sib_recv.at[1])
     for d in ORDER[5:]:
@@ -336,11 +339,20 @@
     elb[0, 8:, :] = jnp.broadcast_to(high[:, :128], (8, 128))
     elb[1, 8:, :] = jnp.broadcast_to(high[:, 128:], (8, 128))
 
-    relay(0)
+    @pl.when(c == 0)
+    def _():
+        relay(0)
+        first_sends(1)
+
+    @pl.when(c == 1)
+    def _():
+        arrived(0, 0, 0)
+        first_sends(1)
+        relay(0)
 
     def add_all(it):
         if it == 0:
-            arrived(it, 0, other)
+            pl.when(c == 0)(lambda: arrived(0, 0, 1))
         add_chip(it, 0)
         for d in (1, -1):
             arrived(it, d, 0)
@@ -375,14 +387,13 @@
             remote(part, part, ag_send.at[1], ag_recv.at[1, y * 2 + h], at_chip(d, c)).start()
     remote(pown.at[other], sib.at[0], sp_send.at[0], sp_recv.at[0], here).start()
     pp_row = row_of(pp)
-    share_scalars(0, jnp.concatenate(
-        [gg_row, pp_row, gp_row * (1.0 / N_SRC), jnp.zeros((5, 128), F32)], axis=0))
+    share_scalars(0, jnp.concatenate([gg_row, pp_row, gp_row * (1.0 / N_SRC)], axis=1))
     acc[...] = jnp.zeros((2, B, 256), F32)
     relay(1)
     add_all(1)
     jp = reduce_src(1)
     sums = sc_out[...]
-    gg, pp, gp = sums[0:1], sums[1:2], sums[2:3]
+    gg, pp, gp = sums[:, :128], sums[:, 128:256], sums[:, 256:]
     alpha0 = gg / (0.5 * gg + gp)
     left = gp / (0.5 * gg + gp)
     rr = alpha0 * (alpha0 * pp - left * gp)
@@ -390,8 +401,8 @@
     scale = left + beta
     alpha0_c, left_c, scale_c = col_of(alpha0), col_of(left), col_of(scale)
     jv = scale_c * j0[...] - alpha0_c * jp
-    scatter_sources(1, jv, lambda: jnp.broadcast_to(row_of(jv * jv), (8, 128)))
-    jj = sum_scalars(1)[0:1]
+    scatter_sources(1, jv, lambda: row_of(jv * jv))
+    jj = sum_scalars(1)
     alpha1 = rr / (0.5 * rr * (1.0 + beta) + jj)
     alpha1_c = col_of(alpha1)
     wait_recv(sib.at[0], sp_recv.at[0])
@@ -414,7 +425,7 @@
         wait_send(gat.at[it, pl.ds(0, 15 - it)], ag_send.at[it])
         wait_send(rs_send.at[it, pl.ds(0, 14)], rs_ssem.at[it])
         wait_send(own.at[it, 0], sp_send.at[it])
-        wait_send(tb.at[it, pl.ds(0, N_RCV - 1)], t_send.at[it])
+        wait_send((tb0, tb1)[it].at[pl.ds(0, N_RCV - 1)], t_send.at[it])
         finish_src(it)
 
 
@@ -445,16 +456,17 @@
             vmem((2, TILES, 16, 128), BF16),
             vmem((2, N_SRC, 16, 128), BF16),
             vmem((2, TILES, 16, 128), BF16),
-            vmem((8, 128), F32),
-            vmem((N_SRC, 8, 128), F32),
-            vmem((8, 128), F32),
+            vmem((1, 384), F32),
+            vmem((N_SRC, 1, 384), F32),
+            vmem((1, 384), F32),
             vmem((2, 16, B, L), BF16),
             vmem((2, 6, B, L), BF16),
             vmem((2, 8, B, L), BF16),
             vmem((2, 2, B, L), F32),
             vmem((2, B, L), F32),
             vmem((2, B, L), F32),
-            vmem((2, N_RCV, 8, 128), F32),
+            vmem((N_RCV, 1, 384), F32),
+            vmem((N_RCV, 1, 128), F32),
             dma((NY,)), dma((NY,)), dma((B // 8,)), dma((4,)), dma((2,)), dma((2,)), dma, dma((NY,)),
             dma((2,)), dma((2, 16)), dma((2,)), dma((2, 6)), dma((2, 8)),
             dma((2,)), dma((2,)), dma((2,)), dma((2,)), dma((2,)), dma((2,)), dma, dma, dma, dma, dma((2,)), dma((2,)),

time: 78.3 us -> 78.4 us (level)
  no operation moved by 1% of the time
where the time goes in v6:
time: 78.4 us; the launch traced here: 78.2 us
  Pallas kernels  76.3 us (97%)
  local copies, waits for them, and re-layouts  1.28 us (2%)
    pallas_call x1, Pallas kernels, shards(): pl.pallas_call(kernel, out_shape=(out, out), in_specs=[pl.BlockSpec(memor...  76.3 us

profile of v6, /device:TPU:1, one launch (start us, length us, event | category | flops | bytes accessed | tf_op | source)
XLA Modules:
  0.0 78.2 jit_solution(10190734061674554637)
XLA Ops:
  0.6 76.3 %shard_map.77 = (f32[48,2,256]{2,1,0:T(2,128)S(1)}, f32[48,2,256]{2,1,0:T(2,128)S(1)}) custom-call(bf16[2,4096,128]{2,1,0:T(8,128)(2,1)} %k_hbm.1, f32[48,2,256]{2,1,0:T(2,128)} %g_hbm.1, f32[48,2,128]{2,1,0:T(2,128)} %tr_hbm.1, f32[48,128]{1,0:T(8,128)} %op_hbm.1, s32[48,128]{1,0:T(8,128)} %st_hbm.1, s32[1,128]{1,0:T(1,128)} %bitcast.1), custom_call_target="tpu_custom_call" | custom-call | flops 805306368 | bytes 4194304 | tf_op jit(solution)/shard_map/pallas_call | solution.py:435
  76.9 0.6 copy.10
  77.6 0.6 copy.11

commit v7 on v6

--- a/solution.py
+++ b/solution.py
@@ -24,10 +24,10 @@
 def kernel(k_hbm, g_hbm, tr_hbm, op_hbm, st_hbm, el_hbm, x_ref, r_ref,
            g_ref, tr_ref, op_ref, st_ref, el_ref,
            kw, k_own, low, elb, co, co_send, sb, gat, acc, j0, ar_s, ar_in, ar_out, sc_s, sc_in, sc_out,
-           rs_send, rs_in, rs_fin, own, pown, sib, tb0, tb1,
-           k_sem, ka_sem, g_sem, in_sem, sib_send, sib_recv, kp_send, kp_recv, ag_send, ag_recv, rs_ssem, rs_recv, rf_recv,
+           rs_send, rs_in, rs_fin, own, pown, sib, tf0, tf1, ts0, ts1, tb0, tb1,
+           k_sem, g_sem, in_sem, sib_send, sib_recv, kp_send, kp_recv, ag_send, ag_recv, rs_ssem, rs_recv, rf_recv,
            sp_send, sp_recv, a1_send, a1_recv, a2_send, a2_recv,
-           s1_send, s1_recv, s2_send, s2_recv, t_send, t_recv):
+           s1_send, s1_recv, s2_send, s2_recv, t_send, t_recv, tc_send, tc_recv):
     src = lax.axis_index("src")
     rcv = lax.axis_index("rcv")
     y = rcv // 2
@@ -53,7 +53,7 @@
         remote(ref, ref, sem, sem, here).wait_send()
 
     g_loads = [
-        pltpu.make_async_copy(g_hbm.at[pl.ds(8 * i, 8)], g_ref.at[pl.ds(8 * i, 8)], g_sem.at[i]) for i in range(B // 8)]
+        pltpu.make_async_copy(g_hbm.at[pl.ds(24 * i, 24)], g_ref.at[pl.ds(24 * i, 24)], g_sem.at[i]) for i in range(2)]
     for load in g_loads:
         load.start()
     loads = [
@@ -83,15 +83,10 @@
     def k_rows(d):
         return pl.ds(pl.multiple_of(chip(d) * (2 * L), 2 * L), 2 * L)
 
-    def k_away(d):
-        return pltpu.make_async_copy(k_hbm.at[other, k_rows(d)], k_own.at[k_rows(d)], ka_sem.at[chip(d)])
-
-    def k_copy(d):
-        return pltpu.make_async_copy(k_hbm.at[c, k_rows(d)], kw.at[c, k_rows(d)], k_sem.at[chip(d)])
-
-    for d in ORDER:
-        k_away(d).start()
-        k_copy(d).start()
+    k_away = pltpu.make_async_copy(k_hbm.at[other], k_own, k_sem.at[0])
+    k_copy = pltpu.make_async_copy(k_hbm.at[c], kw.at[c], k_sem.at[1])
+    k_away.start()
+    k_copy.start()
 
     lane = lax.broadcasted_iota(jnp.int32, (B, 128), 1)
     case = lax.broadcasted_iota(jnp.int32, (B, 128), 0)
@@ -126,22 +121,27 @@
     first_sends(0)
 
     def share_k(d):
-        k_away(d).wait()
         remote(k_own.at[k_rows(d)], kw.at[c, k_rows(d)], kp_send, kp_recv.at[chip(d)], here).start()
 
-    def arrived(it, d, h):
+    def one_arrived(it, d, h):
         slot = chip(d) * 2 + h
         wait_recv(gat.at[it, slot], ag_recv.at[it, slot])
 
+    def arrived(it, d):
+        if d == 4 or (it == 0 and abs(d) < 3):
+            one_arrived(it, d, 0)
+            one_arrived(it, d, 1)
+        else:
+            slot = chip(d) * 2
+            wait_recv(gat.at[it, pl.ds(slot, 2)], ag_recv.at[it, slot])
+
     def relay(it):
-        for h in range(2):
-            for d in (1, -1):
-                arrived(it, -2 * d, h)
-                slot = chip(-2 * d) * 2 + h
-                part = gat.at[it, slot]
-                if (d == 1) == (h == 0):
-                    remote(part, part, ag_send.at[it], ag_recv.at[it, slot], at_chip(2 * d, c)).start()
-                remote(part, part, ag_send.at[it], ag_recv.at[it, slot], at_chip(d, c)).start()
+        for h, d in ((0, 1), (1, -1)):
+            arrived(it, -2 * d)
+            slot = chip(-2 * d) * 2
+            half, both = gat.at[it, slot + h], gat.at[it, pl.ds(slot, 2)]
+            remote(half, half, ag_send.at[it], ag_recv.at[it, slot + h], at_chip(2 * d, c)).start()
+            remote(both, both, ag_send.at[it], ag_recv.at[it, slot], at_chip(d, c)).start()
 
     def block(q):
         rows = pl.ds(pl.multiple_of(q * (2 * L), 2 * L), 2 * L)
@@ -150,7 +150,6 @@
     def add_chip(it, d):
         q = chip(d)
         if it == 0:
-            k_copy(d).wait()
             wait_recv(kw.at[other, k_rows(d)], kp_recv.at[q])
         v0, v1 = gat[it, q * 2], gat[it, q * 2 + 1]
         acc[0] += jnp.dot(jnp.concatenate([v0, v1], axis=1), block(q), preferred_element_type=F32)
@@ -233,19 +232,25 @@
             pl.when(sums_scalars)(lambda: wait_send(sc_in.at[pl.ds(0, N_SRC - 1)], s2_send))
             pl.when(jnp.logical_not(sums_scalars))(lambda: wait_send(sc_s, s1_send))
 
-    def share_scalars(it, row):
-        tb = (tb0, tb1)[it]
-        tb[rcv] = row
+    def share_with_core(it, row):
+        mine, others_row = (tf0, tf1)[it], (ts0, ts1)[it]
+        mine[...] = row
+        remote(mine, others_row, tc_send.at[it], tc_recv.at[it], here).start()
+
+    def share_along_y(it):
+        mine, others_row, tb = (tf0, tf1)[it], (ts0, ts1)[it], (tb0, tb1)[it]
+        wait_recv(others_row, tc_recv.at[it])
+        tb[y] = mine[...] + others_row[...]
 
         def send(d, carry):
-            remote(tb.at[rcv], tb.at[rcv], t_send.at[it], t_recv.at[it], (src, lax.rem(rcv + d, N_RCV))).start()
+            remote(tb.at[y], tb.at[y], t_send.at[it], t_recv.at[it], at_chip(d, c)).start()
             return carry
 
-        lax.fori_loop(1, N_RCV, send, 0)
+        lax.fori_loop(1, NY, send, 0)
 
     def sum_scalars(it):
         tb = (tb0, tb1)[it]
-        wait_recv(tb.at[pl.ds(0, N_RCV - 1)], t_recv.at[it])
+        wait_recv(tb.at[pl.ds(0, NY - 1)], t_recv.at[it])
         return jnp.sum(tb[...], axis=0)
 
     def scatter_sources(it, jv, scalars=None):
@@ -261,49 +266,68 @@
             spread = dot_nt(sparse.astype(BF16), low[...])
             return both[:, :L] + spread[:B], both[:, L:] + spread[B:]
 
-        def send(slot, value, to, landing):
+        def put(slot, value):
             rs_send[it, slot] = value.astype(BF16)
-            remote(rs_send.at[it, slot], rs_in.at[it, landing], rs_ssem.at[it], rs_recv.at[it, landing],
-                   at_chip(to, c)).start()
-
-        def home(slot, value, d, h):
-            rs_send[it, slot] = value.astype(BF16)
-            landing = {1: 0, -1: 2, 2: 4, -2: 6}[d] + (h if it == 0 else c)
-            remote(rs_send.at[it, slot], rs_fin.at[it, landing], rs_ssem.at[it], rf_recv.at[it, landing],
-                   at_chip(d, c if it == 0 else h)).start()
-
-        def came(landing):
-            wait_recv(rs_in.at[it, landing], rs_recv.at[it, landing])
-            return rs_in[it, landing].astype(F32)
+
+        def onward(slot, n, to):
+            part, landing = rs_send.at[it, pl.ds(slot, n)], rs_in.at[it, pl.ds(slot, n)]
+            remote(part, landing, rs_ssem.at[it], rs_recv.at[it, slot], at_chip(to, c)).start()
+
+        def home(slot, d):
+            landing = {1: 0, -1: 2, 2: 4, -2: 6}[d]
+            if it == 0:
+                remote(rs_send.at[it, pl.ds(slot, 2)], rs_fin.at[it, pl.ds(landing, 2)], rs_ssem.at[it],
+                       rf_recv.at[it, landing], at_chip(d, c)).start()
+            else:
+                for h in range(2):
+                    remote(rs_send.at[it, slot + h], rs_fin.at[it, landing + c], rs_ssem.at[it],
+                           rf_recv.at[it, landing + c], at_chip(d, h)).start()
 
         for k, d in enumerate((1, -1)):
             far = part(3 * d)
-            send(2 + 2 * k, far[0], d, 2 + 2 * k)
-            send(3 + 2 * k, far[1], d, 3 + 2 * k)
+            put(2 + 2 * k, far[0])
+            put(3 + 2 * k, far[1])
+            onward(2 + 2 * k, 2, d)
         far = part(4)
-        send(0, far[0], 2, 0)
-        send(1, far[1], -2, 1)
+        put(0, far[0])
+        put(1, far[1])
+        onward(0, 1, 2)
+        onward(1, 1, -2)
         for k, d in enumerate((1, -1)):
             near = part(d)
-            home(6 + 2 * k, near[0], d, 0)
-            home(7 + 2 * k, near[1], d, 1)
+            put(6 + 2 * k, near[0])
+            put(7 + 2 * k, near[1])
+            home(6 + 2 * k, d)
         if scalars is not None:
-            share_scalars(it, scalars())
+            share_with_core(it, scalars())
         up, down, mine = part(2), part(-2), part(0)
         own[it, 0] = mine[0]
         own[it, 1] = mine[1]
         if it == 1:
             remote(own.at[it, other], sib.at[it], sp_send.at[it], sp_recv.at[it], here).start()
-        home(10, up[1] + came(3), 2, 1)
-        home(11, down[0] + came(4), -2, 0)
-        home(12, up[0] + came(2) + came(0), 2, 0)
-        home(13, down[1] + came(5) + came(1), -2, 1)
+
+        def came(slot):
+            return rs_in[it, slot].astype(F32)
+
+        wait_recv(rs_in.at[it, pl.ds(2, 2)], rs_recv.at[it, 2])
+        wait_recv(rs_in.at[it, pl.ds(0, 1)], rs_recv.at[it, 0])
+        put(10, up[0] + came(2) + came(0))
+        put(11, up[1] + came(3))
+        home(10, 2)
+        wait_recv(rs_in.at[it, pl.ds(4, 2)], rs_recv.at[it, 4])
+        wait_recv(rs_in.at[it, pl.ds(1, 1)], rs_recv.at[it, 1])
+        put(12, down[0] + came(4))
+        put(13, down[1] + came(5) + came(1))
+        home(12, -2)
+        if scalars is not None:
+            share_along_y(it)
 
     def arrivals(it, i):
         total = 0.0
         for way in range(4):
             slot = way * 2 + i
-            wait_recv(rs_fin.at[it, slot], rf_recv.at[it, slot])
+            if it == 1:
+                wait_recv(rs_fin.at[it, slot], rf_recv.at[it, slot])
             total += rs_fin[it, slot].astype(F32)
         return total
 
@@ -326,8 +350,10 @@
     co_share.start()
     el_share = remote(elb.at[c, pl.ds(0, 8)], elb.at[c, pl.ds(0, 8)], sib_send.at[1], sib_recv.at[1], here)
     el_share.start()
+    k_away.wait()
     for d in ORDER[:5]:
         share_k(d)
+    first_sends(1)
     acc[...] = jnp.zeros((2, B, 256), F32)
     wait_recv(elb.at[other, pl.ds(0, 8)], sib_recv.at[1])
     for d in ORDER[5:]:
@@ -339,30 +365,16 @@
     elb[0, 8:, :] = jnp.broadcast_to(high[:, :128], (8, 128))
     elb[1, 8:, :] = jnp.broadcast_to(high[:, 128:], (8, 128))
 
-    @pl.when(c == 0)
-    def _():
-        relay(0)
-        first_sends(1)
-
-    @pl.when(c == 1)
-    def _():
-        arrived(0, 0, 0)
-        first_sends(1)
-        relay(0)
+    relay(0)
+    k_copy.wait()
 
     def add_all(it):
         if it == 0:
-            pl.when(c == 0)(lambda: arrived(0, 0, 1))
+            one_arrived(it, 0, other)
         add_chip(it, 0)
-        for d in (1, -1):
-            arrived(it, d, 0)
-            arrived(it, d, 1)
-            add_chip(it, d)
-        for d in (2, -2):
-            add_chip(it, d)
-        for d in (3, -3, 4):
-            arrived(it, d, 0)
-            arrived(it, d, 1)
+        for d in ORDER[1:]:
+            if abs(d) != 2:
+                arrived(it, d)
             add_chip(it, d)
 
     add_all(0)
@@ -373,23 +385,22 @@
     gp_row = row_of(jv * jv)
 
     pp = 0.0
+    for way in range(4):
+        wait_recv(rs_fin.at[0, pl.ds(2 * way, 2)], rf_recv.at[0, 2 * way])
     for h in range(2):
         p = own[0, h] + arrivals(0, h)
         pown[h] = p
         pp += p * p
-        part = gat.at[1, y * 2 + h]
-        part[...] = p.astype(BF16)
-        for d in (2, -2):
-            remote(part, part, ag_send.at[1], ag_recv.at[1, y * 2 + h], at_chip(d, c)).start()
-    for h in range(2):
-        part = gat.at[1, y * 2 + h]
-        for d in (1, -1):
-            remote(part, part, ag_send.at[1], ag_recv.at[1, y * 2 + h], at_chip(d, c)).start()
+        gat[1, y * 2 + h] = p.astype(BF16)
+    both = gat.at[1, pl.ds(y * 2, 2)]
+    for d in (2, -2, 1, -1):
+        remote(both, both, ag_send.at[1], ag_recv.at[1, y * 2], at_chip(d, c)).start()
     remote(pown.at[other], sib.at[0], sp_send.at[0], sp_recv.at[0], here).start()
     pp_row = row_of(pp)
-    share_scalars(0, jnp.concatenate([gg_row, pp_row, gp_row * (1.0 / N_SRC)], axis=1))
+    share_with_core(0, jnp.concatenate([gg_row, pp_row, gp_row * (1.0 / N_SRC)], axis=1))
     acc[...] = jnp.zeros((2, B, 256), F32)
     relay(1)
+    share_along_y(0)
     add_all(1)
     jp = reduce_src(1)
     sums = sc_out[...]
@@ -425,7 +436,8 @@
         wait_send(gat.at[it, pl.ds(0, 15 - it)], ag_send.at[it])
         wait_send(rs_send.at[it, pl.ds(0, 14)], rs_ssem.at[it])
         wait_send(own.at[it, 0], sp_send.at[it])
-        wait_send((tb0, tb1)[it].at[pl.ds(0, N_RCV - 1)], t_send.at[it])
+        wait_send((tb0, tb1)[it].at[pl.ds(0, NY - 1)], t_send.at[it])
+        wait_send((tf0, tf1)[it], tc_send.at[it])
         finish_src(it)
 
 
@@ -465,11 +477,16 @@
             vmem((2, 2, B, L), F32),
             vmem((2, B, L), F32),
             vmem((2, B, L), F32),
-            vmem((N_RCV, 1, 384), F32),
-            vmem((N_RCV, 1, 128), F32),
-            dma((NY,)), dma((NY,)), dma((B // 8,)), dma((4,)), dma((2,)), dma((2,)), dma, dma((NY,)),
+            vmem((1, 384), F32),
+            vmem((1, 128), F32),
+            vmem((1, 384), F32),
+            vmem((1, 128), F32),
+            vmem((NY, 1, 384), F32),
+            vmem((NY, 1, 128), F32),
+            dma((2,)), dma((2,)), dma((4,)), dma((2,)), dma((2,)), dma, dma((NY,)),
             dma((2,)), dma((2, 16)), dma((2,)), dma((2, 6)), dma((2, 8)),
             dma((2,)), dma((2,)), dma((2,)), dma((2,)), dma((2,)), dma((2,)), dma, dma, dma, dma, dma((2,)), dma((2,)),
+            dma((2,)), dma((2,)),
         ],
         compiler_params=pltpu.CompilerParams(
             collective_id=0, has_side_effects=True, vmem_limit_bytes=24 * 1024 * 1024),

time: 78.4 us -> 80.9 us (1.032)
  the two profiles are of different devices: /device:TPU:1 before, /device:TPU:8 now
where the time goes in v7:
time: 80.9 us; the launch traced here: 80.7 us
  Pallas kernels  78.8 us (97%)
  local copies, waits for them, and re-layouts  1.28 us (2%)
    pallas_call x1, Pallas kernels, shards(): pl.pallas_call(kernel, out_shape=(out, out), in_specs=[pl.BlockSpec(memor...  78.8 us

profile of v7, /device:TPU:8, one launch (start us, length us, event | category | flops | bytes accessed | tf_op | source)
XLA Modules:
  0.0 80.7 jit_solution(16703823323784958180)
XLA Ops:
  0.6 78.8 %shard_map.77 = (f32[48,2,256]{2,1,0:T(2,128)S(1)}, f32[48,2,256]{2,1,0:T(2,128)S(1)}) custom-call(bf16[2,4096,128]{2,1,0:T(8,128)(2,1)} %k_hbm.1, f32[48,2,256]{2,1,0:T(2,128)} %g_hbm.1, f32[48,2,128]{2,1,0:T(2,128)} %tr_hbm.1, f32[48,128]{1,0:T(8,128)} %op_hbm.1, s32[48,128]{1,0:T(8,128)} %st_hbm.1, s32[1,128]{1,0:T(1,128)} %bitcast.1), custom_call_target="tpu_custom_call" | custom-call | flops 805306368 | bytes 4194304 | tf_op jit(solution)/shard_map/pallas_call | solution.py:447
  79.4 0.6 copy.10
  80.0 0.6 copy.11

commit v8 on v6

--- a/solution.py
+++ b/solution.py
@@ -15,6 +15,10 @@
 N_SRC = 32
 TILES = 6
 ORDER = (0, 1, -1, 2, -2, 3, -3, 4)
+
+
+def far(i, n):
+    return n // 2 + (i + 1) // 2 * (2 * ((i + 1) % 2) - 1)
 
 
 def dot_nt(a, b):
@@ -69,16 +73,17 @@
     def greet(dev):
         pl.semaphore_signal(barrier, inc=1, device_id=dev, device_id_type=MESH)
 
-    def greet_rcv(d, carry):
-        greet((src, lax.rem(rcv + d, N_RCV)))
+    def greet_src(i):
+        greet((lax.rem(src + far(i, N_SRC), N_SRC), rcv))
+
+    def greet_some(i, carry):
+        greet((src, lax.rem(rcv + far(i, N_RCV), N_RCV)))
+        greet_src(2 * i)
+        greet_src(2 * i + 1)
         return carry
 
-    def greet_src(d, carry):
-        greet((lax.rem(src + d, N_SRC), rcv))
-        return carry
-
-    lax.fori_loop(1, N_RCV, greet_rcv, 0)
-    lax.fori_loop(1, N_SRC, greet_src, 0)
+    lax.fori_loop(0, N_RCV - 1, greet_some, 0)
+    greet_src(N_SRC - 2)
 
     def k_rows(d):
         return pl.ds(pl.multiple_of(chip(d) * (2 * L), 2 * L), 2 * L)
@@ -163,11 +168,11 @@
         return jnp.concatenate([co[0, i], co[1, i]], axis=1)
 
     def others(send):
-        def one(d, carry):
-            send((lax.rem(src + d, N_SRC), rcv))
+        def one(i, carry):
+            send((lax.rem(src + far(i, N_SRC), N_SRC), rcv))
             return carry
 
-        lax.fori_loop(1, N_SRC, one, 0)
+        lax.fori_loop(0, N_SRC - 1, one, 0)
 
     tile = (src - 2 * c + 5) // 5 - 1
     sums_tile = (lax.rem(src - 2 * c + 5, 5) == 0) & (tile >= 0) & (tile < TILES)
@@ -237,11 +242,12 @@
         tb = (tb0, tb1)[it]
         tb[rcv] = row
 
-        def send(d, carry):
-            remote(tb.at[rcv], tb.at[rcv], t_send.at[it], t_recv.at[it], (src, lax.rem(rcv + d, N_RCV))).start()
+        def send(i, carry):
+            remote(tb.at[rcv], tb.at[rcv], t_send.at[it], t_recv.at[it],
+                   (src, lax.rem(rcv + far(i, N_RCV), N_RCV))).start()
             return carry
 
-        lax.fori_loop(1, N_RCV, send, 0)
+        lax.fori_loop(0, N_RCV - 1, send, 0)
 
     def sum_scalars(it):
         tb = (tb0, tb1)[it]
@@ -328,6 +334,7 @@
     el_share.start()
     for d in ORDER[:5]:
         share_k(d)
+    first_sends(1)
     acc[...] = jnp.zeros((2, B, 256), F32)
     wait_recv(elb.at[other, pl.ds(0, 8)], sib_recv.at[1])
     for d in ORDER[5:]:
@@ -339,20 +346,11 @@
     elb[0, 8:, :] = jnp.broadcast_to(high[:, :128], (8, 128))
     elb[1, 8:, :] = jnp.broadcast_to(high[:, 128:], (8, 128))
 
-    @pl.when(c == 0)
-    def _():
-        relay(0)
-        first_sends(1)
-
-    @pl.when(c == 1)
-    def _():
-        arrived(0, 0, 0)
-        first_sends(1)
-        relay(0)
+    relay(0)
 
     def add_all(it):
         if it == 0:
-            pl.when(c == 0)(lambda: arrived(0, 0, 1))
+            arrived(it, 0, other)
         add_chip(it, 0)
         for d in (1, -1):
             arrived(it, d, 0)

time: 78.4 us -> 78 us (level)
  no operation moved by 1% of the time
where the time goes in v8:
time: 78 us; the launch traced here: 77.8 us
  Pallas kernels  75.9 us (97%)
  local copies, waits for them, and re-layouts  1.28 us (2%)
    pallas_call x1, Pallas kernels, shards(): pl.pallas_call(kernel, out_shape=(out, out), in_specs=[pl.BlockSpec(memor...  75.9 us

profile of v8, /device:TPU:1, one launch (start us, length us, event | category | flops | bytes accessed | tf_op | source)
XLA Modules:
  0.0 77.8 jit_solution(13736108968972123025)
XLA Ops:
  0.6 75.9 %shard_map.77 = (f32[48,2,256]{2,1,0:T(2,128)S(1)}, f32[48,2,256]{2,1,0:T(2,128)S(1)}) custom-call(bf16[2,4096,128]{2,1,0:T(8,128)(2,1)} %k_hbm.1, f32[48,2,256]{2,1,0:T(2,128)} %g_hbm.1, f32[48,2,128]{2,1,0:T(2,128)} %tr_hbm.1, f32[48,128]{1,0:T(8,128)} %op_hbm.1, s32[48,128]{1,0:T(8,128)} %st_hbm.1, s32[1,128]{1,0:T(1,128)} %bitcast.1), custom_call_target="tpu_custom_call" | custom-call | flops 805306368 | bytes 4194304 | tf_op jit(solution)/shard_map/pallas_call | solution.py:433
  76.6 0.6 copy.10
  77.2 0.6 copy.11

commit v9 on v8

--- a/solution.py
+++ b/solution.py
@@ -13,6 +13,8 @@
 NY = 8
 N_RCV = 16
 N_SRC = 32
+NX = 4
+NZ = 8
 TILES = 6
 ORDER = (0, 1, -1, 2, -2, 3, -3, 4)
 
@@ -167,16 +169,28 @@
     def coef(i):
         return jnp.concatenate([co[0, i], co[1, i]], axis=1)
 
-    def others(send):
-        def one(i, carry):
-            send((lax.rem(src + far(i, N_SRC), N_SRC), rcv))
-            return carry
-
-        lax.fori_loop(0, N_SRC - 1, one, 0)
-
-    tile = (src - 2 * c + 5) // 5 - 1
-    sums_tile = (lax.rem(src - 2 * c + 5, 5) == 0) & (tile >= 0) & (tile < TILES)
-    sums_scalars = src == 30 + c
+    z = src // NX
+    x = lax.rem(src, NX)
+    tile = lax.rem(z + 4 * (x // 2), NZ)
+    sums_tile = (lax.rem(x, 2) == c) & (tile < TILES)
+    sums_scalars = (lax.rem(x, 2) == c) & (tile == TILES)
+    steps = [(dz, dx) for dz in range(NZ) for dx in range(NX)]
+    reach = {(dz, dx): min(dz, NZ - dz) + min(dx, NX - dx) for dz, dx in steps}
+    near = [s for s in steps if 0 < reach[s] < 3 or (reach[s] == 3 and 0 < s[0] < 4)]
+    near = sorted(near, key=lambda s: -reach[s])
+
+    def send_sum(part, send_sem, recv_sem):
+        for dz, dx in near:
+            dev = (lax.rem(z + dz, NZ) * NX + lax.rem(x + dx, NX), rcv)
+            remote(part, part, send_sem, recv_sem, dev).start()
+
+    def send_to_sums(t, part, landing, send_sem, recv_sem):
+        for end in range(2):
+            owner = lax.rem(t + 4 * end, NZ) * NX + c + 2 * end
+
+            @pl.when(owner != src)
+            def _():
+                remote(part, landing.at[src], send_sem, recv_sem, (owner, rcv)).start()
 
     def reduce_src(it):
         part = (coef(0) * acc[1] + coef(1) * acc[0]).astype(BF16)
@@ -184,35 +198,27 @@
             ar_s[it, 3 * half:3 * half + 3] = part[:, 128 * half:128 * half + 128].reshape(3, 16, 128)
 
         def send(t, carry):
-            owner = 5 * t + 2 * c
-
-            @pl.when(owner != src)
-            def _():
-                remote(ar_s.at[it, t], ar_in.at[it, src], a1_send.at[it], a1_recv.at[it], (owner, rcv)).start()
+            send_to_sums(t, ar_s.at[it, t], ar_in.at[it], a1_send.at[it], a1_recv.at[it])
             return carry
 
         lax.fori_loop(0, TILES, send, 0)
         if it == 1:
             sc_s[...] = sum_scalars(0)
-
-            @pl.when(jnp.logical_not(sums_scalars))
-            def _():
-                remote(sc_s, sc_in.at[src], s1_send, s1_recv, (30 + c, rcv)).start()
+            send_to_sums(TILES, sc_s, sc_in, s1_send, s1_recv)
 
             @pl.when(sums_scalars)
             def _():
                 sc_in[src] = sc_s[...]
                 wait_recv(sc_in.at[pl.ds(0, N_SRC - 1)], s1_recv)
                 sc_out[...] = jnp.sum(sc_in[...], axis=0)
-                others(lambda dev: remote(sc_out, sc_out, s2_send, s2_recv, dev).start())
+                send_sum(sc_out, s2_send, s2_recv)
 
         @pl.when(sums_tile)
         def _():
             ar_in[it, src] = ar_s[it, tile]
             wait_recv(ar_in.at[it, pl.ds(0, N_SRC - 1)], a1_recv.at[it])
             ar_out[it, tile] = jnp.sum(ar_in[it].astype(F32), axis=0).astype(BF16)
-            part = ar_out.at[it, tile]
-            others(lambda dev: remote(part, part, a2_send.at[it], a2_recv.at[it], dev).start())
+            send_sum(ar_out.at[it, tile], a2_send.at[it], a2_recv.at[it])
             wait_recv(ar_out.at[it, pl.ds(0, TILES - 1)], a2_recv.at[it])
 
         @pl.when(jnp.logical_not(sums_tile))
@@ -227,16 +233,22 @@
     def finish_src(it):
         @pl.when(sums_tile)
         def _():
-            wait_send(ar_in.at[it, pl.ds(0, N_SRC - 1)], a2_send.at[it])
-            wait_send(ar_s.at[it, pl.ds(0, TILES - 1)], a1_send.at[it])
+            wait_send(ar_in.at[it, pl.ds(0, len(near))], a2_send.at[it])
+            wait_send(ar_in.at[it, pl.ds(0, 2 * TILES - 1)], a1_send.at[it])
 
         @pl.when(jnp.logical_not(sums_tile))
         def _():
-            wait_send(ar_s.at[it, pl.ds(0, TILES)], a1_send.at[it])
+            wait_send(ar_in.at[it, pl.ds(0, 2 * TILES)], a1_send.at[it])
 
         if it == 1:
-            pl.when(sums_scalars)(lambda: wait_send(sc_in.at[pl.ds(0, N_SRC - 1)], s2_send))
-            pl.when(jnp.logical_not(sums_scalars))(lambda: wait_send(sc_s, s1_send))
+            @pl.when(sums_scalars)
+            def _():
+                wait_send(sc_in.at[pl.ds(0, len(near))], s2_send)
+                wait_send(sc_in.at[pl.ds(0, 1)], s1_send)
+
+            @pl.when(jnp.logical_not(sums_scalars))
+            def _():
+                wait_send(sc_in.at[pl.ds(0, 2)], s1_send)
 
     def share_scalars(it, row):
         tb = (tb0, tb1)[it]
@@ -282,13 +294,13 @@
             wait_recv(rs_in.at[it, landing], rs_recv.at[it, landing])
             return rs_in[it, landing].astype(F32)
 
+        far = part(4)
+        send(0, far[0], 2, 0)
+        send(1, far[1], -2, 1)
         for k, d in enumerate((1, -1)):
             far = part(3 * d)
             send(2 + 2 * k, far[0], d, 2 + 2 * k)
             send(3 + 2 * k, far[1], d, 3 + 2 * k)
-        far = part(4)
-        send(0, far[0], 2, 0)
-        send(1, far[1], -2, 1)
         for k, d in enumerate((1, -1)):
             near = part(d)
             home(6 + 2 * k, near[0], d, 0)

time: 78 us -> 77.3 us (level)
  no operation moved by 1% of the time
where the time goes in v9:
time: 77.3 us; the launch traced here: 77.2 us
  Pallas kernels  75.2 us (97%)
  local copies, waits for them, and re-layouts  1.28 us (2%)
    pallas_call x1, Pallas kernels, shards(): pl.pallas_call(kernel, out_shape=(out, out), in_specs=[pl.BlockSpec(memor...  75.2 us

profile of v9, /device:TPU:1, one launch (start us, length us, event | category | flops | bytes accessed | tf_op | source)
XLA Modules:
  0.0 77.2 jit_solution(4360260593229741829)
XLA Ops:
  0.6 75.2 %shard_map.77 = (f32[48,2,256]{2,1,0:T(2,128)S(1)}, f32[48,2,256]{2,1,0:T(2,128)S(1)}) custom-call(bf16[2,4096,128]{2,1,0:T(8,128)(2,1)} %k_hbm.1, f32[48,2,256]{2,1,0:T(2,128)} %g_hbm.1, f32[48,2,128]{2,1,0:T(2,128)} %tr_hbm.1, f32[48,128]{1,0:T(8,128)} %op_hbm.1, s32[48,128]{1,0:T(8,128)} %st_hbm.1, s32[1,128]{1,0:T(1,128)} %bitcast.1), custom_call_target="tpu_custom_call" | custom-call | flops 805306368 | bytes 4194304 | tf_op jit(solution)/shard_map/pallas_call | solution.py:445
  75.9 0.6 copy.10
  76.5 0.6 copy.11

commit v10 on v9

--- a/solution.py
+++ b/solution.py
@@ -17,6 +17,7 @@
 NZ = 8
 TILES = 6
 ORDER = (0, 1, -1, 2, -2, 3, -3, 4)
+WAYS = (4, 3, -3, 2, -2, 1, -1)
 
 
 def far(i, n):
@@ -30,8 +31,8 @@
 def kernel(k_hbm, g_hbm, tr_hbm, op_hbm, st_hbm, el_hbm, x_ref, r_ref,
            g_ref, tr_ref, op_ref, st_ref, el_ref,
            kw, k_own, low, elb, co, co_send, sb, gat, acc, j0, ar_s, ar_in, ar_out, sc_s, sc_in, sc_out,
-           rs_send, rs_in, rs_fin, own, pown, sib, tb0, tb1,
-           k_sem, ka_sem, g_sem, in_sem, sib_send, sib_recv, kp_send, kp_recv, ag_send, ag_recv, rs_ssem, rs_recv, rf_recv,
+           rs_send, rs_fin, own, pown, sib, tb0, tb1,
+           k_sem, ka_sem, g_sem, in_sem, sib_send, sib_recv, kp_send, kp_recv, ag_send, ag_recv, rs_ssem, rf_recv,
            sp_send, sp_recv, a1_send, a1_recv, a2_send, a2_recv,
            s1_send, s1_recv, s2_send, s2_recv, t_send, t_recv):
     src = lax.axis_index("src")
@@ -123,7 +124,7 @@
     pl.semaphore_wait(barrier, N_RCV + N_SRC - 2)
 
     def first_sends(comp):
-        for d in (2, -2, 1, -1):
+        for d in WAYS:
             remote(sb.at[comp], gat.at[0, rcv], ag_send.at[0], ag_recv.at[0, rcv], at_chip(d, comp)).start()
 
         @pl.when(c != comp)
@@ -139,16 +140,6 @@
     def arrived(it, d, h):
         slot = chip(d) * 2 + h
         wait_recv(gat.at[it, slot], ag_recv.at[it, slot])
-
-    def relay(it):
-        for h in range(2):
-            for d in (1, -1):
-                arrived(it, -2 * d, h)
-                slot = chip(-2 * d) * 2 + h
-                part = gat.at[it, slot]
-                if (d == 1) == (h == 0):
-                    remote(part, part, ag_send.at[it], ag_recv.at[it, slot], at_chip(2 * d, c)).start()
-                remote(part, part, ag_send.at[it], ag_recv.at[it, slot], at_chip(d, c)).start()
 
     def block(q):
         rows = pl.ds(pl.multiple_of(q * (2 * L), 2 * L), 2 * L)
@@ -279,47 +270,30 @@
             spread = dot_nt(sparse.astype(BF16), low[...])
             return both[:, :L] + spread[:B], both[:, L:] + spread[B:]
 
-        def send(slot, value, to, landing):
-            rs_send[it, slot] = value.astype(BF16)
-            remote(rs_send.at[it, slot], rs_in.at[it, landing], rs_ssem.at[it], rs_recv.at[it, landing],
-                   at_chip(to, c)).start()
-
-        def home(slot, value, d, h):
-            rs_send[it, slot] = value.astype(BF16)
-            landing = {1: 0, -1: 2, 2: 4, -2: 6}[d] + (h if it == 0 else c)
-            remote(rs_send.at[it, slot], rs_fin.at[it, landing], rs_ssem.at[it], rf_recv.at[it, landing],
-                   at_chip(d, c if it == 0 else h)).start()
-
-        def came(landing):
-            wait_recv(rs_in.at[it, landing], rs_recv.at[it, landing])
-            return rs_in[it, landing].astype(F32)
-
-        far = part(4)
-        send(0, far[0], 2, 0)
-        send(1, far[1], -2, 1)
-        for k, d in enumerate((1, -1)):
-            far = part(3 * d)
-            send(2 + 2 * k, far[0], d, 2 + 2 * k)
-            send(3 + 2 * k, far[1], d, 3 + 2 * k)
-        for k, d in enumerate((1, -1)):
-            near = part(d)
-            home(6 + 2 * k, near[0], d, 0)
-            home(7 + 2 * k, near[1], d, 1)
+        def home(d):
+            value = part(d)
+            for h in range(2):
+                slot = 2 * WAYS.index(d) + h
+                landing = 2 * WAYS.index(d) + (h if it == 0 else c)
+                rs_send[it, slot] = value[h].astype(BF16)
+                remote(rs_send.at[it, slot], rs_fin.at[it, landing], rs_ssem.at[it], rf_recv.at[it, landing],
+                       at_chip(d, c if it == 0 else h)).start()
+
+        for d in WAYS[:5]:
+            home(d)
         if scalars is not None:
             share_scalars(it, scalars())
-        up, down, mine = part(2), part(-2), part(0)
+        for d in WAYS[5:]:
+            home(d)
+        mine = part(0)
         own[it, 0] = mine[0]
         own[it, 1] = mine[1]
         if it == 1:
             remote(own.at[it, other], sib.at[it], sp_send.at[it], sp_recv.at[it], here).start()
-        home(10, up[1] + came(3), 2, 1)
-        home(11, down[0] + came(4), -2, 0)
-        home(12, up[0] + came(2) + came(0), 2, 0)
-        home(13, down[1] + came(5) + came(1), -2, 1)
 
     def arrivals(it, i):
         total = 0.0
-        for way in range(4):
+        for way in range(len(WAYS)):
             slot = way * 2 + i
             wait_recv(rs_fin.at[it, slot], rf_recv.at[it, slot])
             total += rs_fin[it, slot].astype(F32)
@@ -358,19 +332,11 @@
     elb[0, 8:, :] = jnp.broadcast_to(high[:, :128], (8, 128))
     elb[1, 8:, :] = jnp.broadcast_to(high[:, 128:], (8, 128))
 
-    relay(0)
-
     def add_all(it):
         if it == 0:
             arrived(it, 0, other)
         add_chip(it, 0)
-        for d in (1, -1):
-            arrived(it, d, 0)
-            arrived(it, d, 1)
-            add_chip(it, d)
-        for d in (2, -2):
-            add_chip(it, d)
-        for d in (3, -3, 4):
+        for d in ORDER[1:]:
             arrived(it, d, 0)
             arrived(it, d, 1)
             add_chip(it, d)
@@ -389,17 +355,12 @@
         pp += p * p
         part = gat.at[1, y * 2 + h]
         part[...] = p.astype(BF16)
-        for d in (2, -2):
-            remote(part, part, ag_send.at[1], ag_recv.at[1, y * 2 + h], at_chip(d, c)).start()
-    for h in range(2):
-        part = gat.at[1, y * 2 + h]
-        for d in (1, -1):
+        for d in WAYS:
             remote(part, part, ag_send.at[1], ag_recv.at[1, y * 2 + h], at_chip(d, c)).start()
     remote(pown.at[other], sib.at[0], sp_send.at[0], sp_recv.at[0], here).start()
     pp_row = row_of(pp)
     share_scalars(0, jnp.concatenate([gg_row, pp_row, gp_row * (1.0 / N_SRC)], axis=1))
     acc[...] = jnp.zeros((2, B, 256), F32)
-    relay(1)
     add_all(1)
     jp = reduce_src(1)
     sums = sc_out[...]
@@ -470,15 +431,14 @@
             vmem((N_SRC, 1, 384), F32),
             vmem((1, 384), F32),
             vmem((2, 16, B, L), BF16),
-            vmem((2, 6, B, L), BF16),
-            vmem((2, 8, B, L), BF16),
+            vmem((2, 14, B, L), BF16),
             vmem((2, 2, B, L), F32),
             vmem((2, B, L), F32),
             vmem((2, B, L), F32),
             vmem((N_RCV, 1, 384), F32),
             vmem((N_RCV, 1, 128), F32),
             dma((NY,)), dma((NY,)), dma((B // 8,)), dma((4,)), dma((2,)), dma((2,)), dma, dma((NY,)),
-            dma((2,)), dma((2, 16)), dma((2,)), dma((2, 6)), dma((2, 8)),
+            dma((2,)), dma((2, 16)), dma((2,)), dma((2, 14)),
             dma((2,)), dma((2,)), dma((2,)), dma((2,)), dma((2,)), dma((2,)), dma, dma, dma, dma, dma((2,)), dma((2,)),
         ],
         compiler_params=pltpu.CompilerParams(

time: 77.3 us -> 82.9 us (1.072)
  Pallas kernels: 75.2 us -> 80.8 us
    pallas_call x1, Pallas kernels: 75.2 us -> 80.8 us  [shards(): pl.pallas_call(kernel, out_shape=(out, out), in_specs=[pl.BlockSpec(memor...]
where the time goes in v10:
time: 82.9 us; the launch traced here: 82.7 us
  Pallas kernels  80.8 us (97%)
  local copies, waits for them, and re-layouts  1.28 us (2%)
    pallas_call x1, Pallas kernels, shards(): pl.pallas_call(kernel, out_shape=(out, out), in_specs=[pl.BlockSpec(memor...  80.8 us

profile of v10, /device:TPU:1, one launch (start us, length us, event | category | flops | bytes accessed | tf_op | source)
XLA Modules:
  0.0 82.7 jit_solution(1798517408401968620)
XLA Ops:
  0.6 80.8 %shard_map.77 = (f32[48,2,256]{2,1,0:T(2,128)S(1)}, f32[48,2,256]{2,1,0:T(2,128)S(1)}) custom-call(bf16[2,4096,128]{2,1,0:T(8,128)(2,1)} %k_hbm.1, f32[48,2,256]{2,1,0:T(2,128)} %g_hbm.1, f32[48,2,128]{2,1,0:T(2,128)} %tr_hbm.1, f32[48,128]{1,0:T(8,128)} %op_hbm.1, s32[48,128]{1,0:T(8,128)} %st_hbm.1, s32[1,128]{1,0:T(1,128)} %bitcast.1), custom_call_target="tpu_custom_call" | custom-call | flops 805306368 | bytes 4194304 | tf_op jit(solution)/shard_map/pallas_call | solution.py:406
  81.4 0.6 copy.10
  82.1 0.6 copy.11

commit v11 on v9

--- a/solution.py
+++ b/solution.py
@@ -154,17 +154,21 @@
         rows = pl.ds(pl.multiple_of(q * (2 * L), 2 * L), 2 * L)
         return jnp.concatenate([kw[0, rows, :], kw[1, rows, :]], axis=1)
 
-    def add_chip(it, d):
-        q = chip(d)
+    def high_bits():
+        return jnp.concatenate([elb[0, 8:9, :], elb[1, 8:9, :]], axis=1)
+
+    def add_chips(it, ds):
         if it == 0:
-            k_copy(d).wait()
-            wait_recv(kw.at[other, k_rows(d)], kp_recv.at[q])
-        v0, v1 = gat[it, q * 2], gat[it, q * 2 + 1]
-        acc[0] += jnp.dot(jnp.concatenate([v0, v1], axis=1), block(q), preferred_element_type=F32)
-        ed = jnp.dot(jnp.concatenate([v0, v1], axis=0), low[...], preferred_element_type=F32)
-        high = elb[:, 8:9, :]
-        high = jnp.concatenate([high[0], high[1]], axis=1)
-        acc[1] += jnp.where(high == q * 2, ed[:B], 0.0) + jnp.where(high == q * 2 + 1, ed[B:], 0.0)
+            for d in ds:
+                k_copy(d).wait()
+                wait_recv(kw.at[other, k_rows(d)], kp_recv.at[chip(d)])
+        slots = [chip(d) * 2 + h for d in ds for h in range(2)]
+        parts = [gat[it, slot] for slot in slots]
+        stiff = jnp.concatenate([block(chip(d)) for d in ds], axis=0)
+        acc[0] += jnp.dot(jnp.concatenate(parts, axis=1), stiff, preferred_element_type=F32)
+        ed = jnp.dot(jnp.concatenate(parts, axis=0), low[...], preferred_element_type=F32)
+        high = high_bits()
+        acc[1] += sum(jnp.where(high == slot, ed[B * k:B * k + B], 0.0) for k, slot in enumerate(slots))
 
     def coef(i):
         return jnp.concatenate([co[0, i], co[1, i]], axis=1)
@@ -269,15 +273,15 @@
     def scatter_sources(it, jv, scalars=None):
         w = (coef(1) * jv).astype(BF16)
         lift = coef(0) * jv
-        high = jnp.concatenate([elb[0, 8:9, :], elb[1, 8:9, :]], axis=1)
-
-        def part(d):
-            q = chip(d)
-            both = dot_nt(w, block(q))
-            sparse = jnp.concatenate(
-                [jnp.where(high == q * 2, lift, 0.0), jnp.where(high == q * 2 + 1, lift, 0.0)], axis=0)
+        high = high_bits()
+
+        def parts(ds):
+            slots = [chip(d) * 2 + h for d in ds for h in range(2)]
+            both = dot_nt(w, jnp.concatenate([block(chip(d)) for d in ds], axis=0))
+            sparse = jnp.concatenate([jnp.where(high == slot, lift, 0.0) for slot in slots], axis=0)
             spread = dot_nt(sparse.astype(BF16), low[...])
-            return both[:, :L] + spread[:B], both[:, L:] + spread[B:]
+            sums = [both[:, L * k:L * k + L] + spread[B * k:B * k + B] for k in range(len(slots))]
+            return [sums[2 * k:2 * k + 2] for k in range(len(ds))]
 
         def send(slot, value, to, landing):
             rs_send[it, slot] = value.astype(BF16)
@@ -294,24 +298,22 @@
             wait_recv(rs_in.at[it, landing], rs_recv.at[it, landing])
             return rs_in[it, landing].astype(F32)
 
-        far = part(4)
-        send(0, far[0], 2, 0)
-        send(1, far[1], -2, 1)
-        for k, d in enumerate((1, -1)):
-            far = part(3 * d)
-            send(2 + 2 * k, far[0], d, 2 + 2 * k)
-            send(3 + 2 * k, far[1], d, 3 + 2 * k)
-        for k, d in enumerate((1, -1)):
-            near = part(d)
-            home(6 + 2 * k, near[0], d, 0)
-            home(7 + 2 * k, near[1], d, 1)
-        if scalars is not None:
-            share_scalars(it, scalars())
-        up, down, mine = part(2), part(-2), part(0)
+        four, three, minus_three = parts((4, 3, -3))
+        send(0, four[0], 2, 0)
+        send(1, four[1], -2, 1)
+        for k, (d, value) in enumerate(((1, three), (-1, minus_three))):
+            send(2 + 2 * k, value[0], d, 2 + 2 * k)
+            send(3 + 2 * k, value[1], d, 3 + 2 * k)
+        one, minus_one, up, down, mine = parts((1, -1, 2, -2, 0))
+        for k, (d, value) in enumerate(((1, one), (-1, minus_one))):
+            home(6 + 2 * k, value[0], d, 0)
+            home(7 + 2 * k, value[1], d, 1)
         own[it, 0] = mine[0]
         own[it, 1] = mine[1]
         if it == 1:
             remote(own.at[it, other], sib.at[it], sp_send.at[it], sp_recv.at[it], here).start()
+        if scalars is not None:
+            share_scalars(it, scalars())
         home(10, up[1] + came(3), 2, 1)
         home(11, down[0] + came(4), -2, 0)
         home(12, up[0] + came(2) + came(0), 2, 0)
@@ -363,17 +365,14 @@
     def add_all(it):
         if it == 0:
             arrived(it, 0, other)
-        add_chip(it, 0)
         for d in (1, -1):
             arrived(it, d, 0)
             arrived(it, d, 1)
-            add_chip(it, d)
-        for d in (2, -2):
-            add_chip(it, d)
-        for d in (3, -3, 4):
+        add_chips(it, ORDER[:5])
+        for d in ORDER[5:]:
             arrived(it, d, 0)
             arrived(it, d, 1)
-            add_chip(it, d)
+        add_chips(it, ORDER[5:])
 
     add_all(0)
     wait_recv(co.at[other], sib_recv.at[0])

time: 77.3 us -> 77.3 us (level)
  no operation moved by 1% of the time
where the time goes in v11:
time: 77.3 us; the launch traced here: 77.1 us
  Pallas kernels  75.2 us (97%)
  local copies, waits for them, and re-layouts  1.28 us (2%)
    pallas_call x1, Pallas kernels, shards(): pl.pallas_call(kernel, out_shape=(out, out), in_specs=[pl.BlockSpec(memor...  75.2 us

profile of v11, /device:TPU:1, one launch (start us, length us, event | category | flops | bytes accessed | tf_op | source)
XLA Modules:
  0.0 77.1 jit_solution(1427939671498591458)
XLA Ops:
  0.6 75.2 %shard_map.77 = (f32[48,2,256]{2,1,0:T(2,128)S(1)}, f32[48,2,256]{2,1,0:T(2,128)S(1)}) custom-call(bf16[2,4096,128]{2,1,0:T(8,128)(2,1)} %k_hbm.1, f32[48,2,256]{2,1,0:T(2,128)} %g_hbm.1, f32[48,2,128]{2,1,0:T(2,128)} %tr_hbm.1, f32[48,128]{1,0:T(8,128)} %op_hbm.1, s32[48,128]{1,0:T(8,128)} %st_hbm.1, s32[1,128]{1,0:T(1,128)} %bitcast.1), custom_call_target="tpu_custom_call" | custom-call | flops 805306368 | bytes 4194304 | tf_op jit(solution)/shard_map/pallas_call | solution.py:444
  75.9 0.6 copy.10
  76.5 0.6 copy.11

commit v12 on v11

--- a/solution.py
+++ b/solution.py
@@ -28,7 +28,7 @@
 
 
 def kernel(k_hbm, g_hbm, tr_hbm, op_hbm, st_hbm, el_hbm, x_ref, r_ref,
-           g_ref, tr_ref, op_ref, st_ref, el_ref,
+           g_ref, g_own, tr_ref, op_ref, st_ref, el_ref,
            kw, k_own, low, elb, co, co_send, sb, gat, acc, j0, ar_s, ar_in, ar_out, sc_s, sc_in, sc_out,
            rs_send, rs_in, rs_fin, own, pown, sib, tb0, tb1,
            k_sem, ka_sem, g_sem, in_sem, sib_send, sib_recv, kp_send, kp_recv, ag_send, ag_recv, rs_ssem, rs_recv, rf_recv,
@@ -39,6 +39,13 @@
     y = rcv // 2
     c = lax.rem(rcv, 2)
     other = 1 - c
+
+    z = src // NX
+    x = lax.rem(src, NX)
+    tile = lax.rem(z + 4 * (x // 2), NZ)
+    sums_tile = (lax.rem(x, 2) == c) & (tile < TILES)
+    sums_scalars = (lax.rem(x, 2) == c) & (tile == TILES)
+    sums = (lax.rem(x, 2) == c) & (tile <= TILES)
 
     def chip(d):
         return lax.rem(y + d + NY, NY)
@@ -76,7 +83,10 @@
         pl.semaphore_signal(barrier, inc=1, device_id=dev, device_id_type=MESH)
 
     def greet_src(i):
-        greet((lax.rem(src + far(i, N_SRC), N_SRC), rcv))
+        to = lax.rem(src + far(i, N_SRC), N_SRC)
+        to_z, to_x = to // NX, lax.rem(to, NX)
+        to_sums = (lax.rem(to_x, 2) == c) & (lax.rem(to_z + 4 * (to_x // 2), NZ) <= TILES)
+        pl.when(sums | to_sums)(lambda: greet((to, rcv)))
 
     def greet_some(i, carry):
         greet((src, lax.rem(rcv + far(i, N_RCV), N_RCV)))
@@ -114,13 +124,16 @@
     for load in g_loads:
         load.wait()
     g0, g1 = g_ref[:, 0, :], g_ref[:, 1, :]
+    g_own[0] = g0
+    g_own[1] = g1
     b0, b1 = g0.astype(BF16), g1.astype(BF16)
     sb[0] = b0
     sb[1] = b1
     gat[0, rcv] = jnp.where(c == 0, b0, b1)
     gg_row = row_of(g0 * g0 + g1 * g1)
 
-    pl.semaphore_wait(barrier, N_RCV + N_SRC - 2)
+    pl.when(sums)(lambda: pl.semaphore_wait(barrier, N_RCV + N_SRC - 2))
+    pl.when(jnp.logical_not(sums))(lambda: pl.semaphore_wait(barrier, N_RCV - 1 + 2 * (TILES + 1)))
 
     def first_sends(comp):
         for d in (2, -2, 1, -1):
@@ -173,11 +186,6 @@
     def coef(i):
         return jnp.concatenate([co[0, i], co[1, i]], axis=1)
 
-    z = src // NX
-    x = lax.rem(src, NX)
-    tile = lax.rem(z + 4 * (x // 2), NZ)
-    sums_tile = (lax.rem(x, 2) == c) & (tile < TILES)
-    sums_scalars = (lax.rem(x, 2) == c) & (tile == TILES)
     steps = [(dz, dx) for dz in range(NZ) for dx in range(NX)]
     reach = {(dz, dx): min(dz, NZ - dz) + min(dx, NX - dx) for dz, dx in steps}
     near = [s for s in steps if 0 < reach[s] < 3 or (reach[s] == 3 and 0 < s[0] < 4)]
@@ -280,8 +288,8 @@
             both = dot_nt(w, jnp.concatenate([block(chip(d)) for d in ds], axis=0))
             sparse = jnp.concatenate([jnp.where(high == slot, lift, 0.0) for slot in slots], axis=0)
             spread = dot_nt(sparse.astype(BF16), low[...])
-            sums = [both[:, L * k:L * k + L] + spread[B * k:B * k + B] for k in range(len(slots))]
-            return [sums[2 * k:2 * k + 2] for k in range(len(ds))]
+            totals = [both[:, L * k:L * k + L] + spread[B * k:B * k + B] for k in range(len(slots))]
+            return [totals[2 * k:2 * k + 2] for k in range(len(ds))]
 
         def send(slot, value, to, landing):
             rs_send[it, slot] = value.astype(BF16)
@@ -327,6 +335,9 @@
             total += rs_fin[it, slot].astype(F32)
         return total
 
+    for d in ORDER[:5]:
+        share_k(d)
+
     for load in loads:
         load.wait()
     tau, press = tr_ref[:, 0, :], tr_ref[:, 1, :]
@@ -346,8 +357,6 @@
     co_share.start()
     el_share = remote(elb.at[c, pl.ds(0, 8)], elb.at[c, pl.ds(0, 8)], sib_send.at[1], sib_recv.at[1], here)
     el_share.start()
-    for d in ORDER[:5]:
-        share_k(d)
     first_sends(1)
     acc[...] = jnp.zeros((2, B, 256), F32)
     wait_recv(elb.at[other, pl.ds(0, 8)], sib_recv.at[1])
@@ -401,8 +410,8 @@
     relay(1)
     add_all(1)
     jp = reduce_src(1)
-    sums = sc_out[...]
-    gg, pp, gp = sums[:, :128], sums[:, 128:256], sums[:, 256:]
+    sc = sc_out[...]
+    gg, pp, gp = sc[:, :128], sc[:, 128:256], sc[:, 256:]
     alpha0 = gg / (0.5 * gg + gp)
     left = gp / (0.5 * gg + gp)
     rr = alpha0 * (alpha0 * pp - left * gp)
@@ -417,7 +426,7 @@
     wait_recv(sib.at[0], sp_recv.at[0])
     base = []
     for comp in range(2):
-        gv = g_ref[:, comp, :]
+        gv = g_own[comp]
         pv = jnp.where(c == comp, pown[c], sib[0])
         direction = scale_c * gv - alpha0_c * pv
         x_ref[:, comp, :] = alpha0_c * gv + alpha1_c * direction
@@ -448,6 +457,7 @@
         out_specs=[pl.BlockSpec(memory_space=pltpu.VMEM)] * 2,
         scratch_shapes=[
             vmem((B, 2, L), F32),
+            vmem((2, B, L), F32),
             vmem((B, 2, 128), F32),
             vmem((B, 128), F32),
             vmem((B, 128), jnp.int32),

time: 77.3 us -> 77.2 us (level)
  no operation moved by 1% of the time
where the time goes in v12:
time: 77.2 us; the launch traced here: 77.1 us
  Pallas kernels  75.2 us (97%)
  local copies, waits for them, and re-layouts  1.28 us (2%)
    pallas_call x1, Pallas kernels, shards(): pl.pallas_call(kernel, out_shape=(out, out), in_specs=[pl.BlockSpec(memor...  75.2 us

profile of v12, /device:TPU:1, one launch (start us, length us, event | category | flops | bytes accessed | tf_op | source)
XLA Modules:
  0.0 77.1 jit_solution(18232279657806694057)
XLA Ops:
  0.6 75.2 %shard_map.77 = (f32[48,2,256]{2,1,0:T(2,128)S(1)}, f32[48,2,256]{2,1,0:T(2,128)S(1)}) custom-call(bf16[2,4096,128]{2,1,0:T(8,128)(2,1)} %k_hbm.1, f32[48,2,256]{2,1,0:T(2,128)} %g_hbm.1, f32[48,2,128]{2,1,0:T(2,128)} %tr_hbm.1, f32[48,128]{1,0:T(8,128)} %op_hbm.1, s32[48,128]{1,0:T(8,128)} %st_hbm.1, s32[1,128]{1,0:T(1,128)} %bitcast.1), custom_call_target="tpu_custom_call" | custom-call | flops 805306368 | bytes 4194304 | tf_op jit(solution)/shard_map/pallas_call | solution.py:453
  75.8 0.6 copy.10
  76.4 0.6 copy.11

commit v13 on v12

--- a/solution.py
+++ b/solution.py
@@ -57,6 +57,10 @@
         return pltpu.make_async_remote_copy(
             src_ref=s, dst_ref=d, send_sem=ss, recv_sem=rs, device_id=dev, device_id_type=MESH)
 
+    def start_rows(s, d, ss, rs, dev):
+        for first in range(0, B, 16):
+            remote(s.at[pl.ds(first, 16)], d.at[pl.ds(first, 16)], ss, rs, dev).start()
+
     here = (src, y * 2 + other)
 
     def wait_recv(ref, sem):
@@ -136,7 +140,9 @@
     pl.when(jnp.logical_not(sums))(lambda: pl.semaphore_wait(barrier, N_RCV - 1 + 2 * (TILES + 1)))
 
     def first_sends(comp):
-        for d in (2, -2, 1, -1):
+        for d in (2, -2):
+            start_rows(sb.at[comp], gat.at[0, rcv], ag_send.at[0], ag_recv.at[0, rcv], at_chip(d, comp))
+        for d in (1, -1):
             remote(sb.at[comp], gat.at[0, rcv], ag_send.at[0], ag_recv.at[0, rcv], at_chip(d, comp)).start()
 
         @pl.when(c != comp)
@@ -160,8 +166,8 @@
                 slot = chip(-2 * d) * 2 + h
                 part = gat.at[it, slot]
                 if (d == 1) == (h == 0):
-                    remote(part, part, ag_send.at[it], ag_recv.at[it, slot], at_chip(2 * d, c)).start()
-                remote(part, part, ag_send.at[it], ag_recv.at[it, slot], at_chip(d, c)).start()
+                    start_rows(part, part, ag_send.at[it], ag_recv.at[it, slot], at_chip(2 * d, c))
+                start_rows(part, part, ag_send.at[it], ag_recv.at[it, slot], at_chip(d, c))
 
     def block(q):
         rows = pl.ds(pl.multiple_of(q * (2 * L), 2 * L), 2 * L)
@@ -293,14 +299,18 @@
 
         def send(slot, value, to, landing):
             rs_send[it, slot] = value.astype(BF16)
-            remote(rs_send.at[it, slot], rs_in.at[it, landing], rs_ssem.at[it], rs_recv.at[it, landing],
-                   at_chip(to, c)).start()
+            start_rows(rs_send.at[it, slot], rs_in.at[it, landing], rs_ssem.at[it], rs_recv.at[it, landing],
+                       at_chip(to, c))
 
         def home(slot, value, d, h):
             rs_send[it, slot] = value.astype(BF16)
             landing = {1: 0, -1: 2, 2: 4, -2: 6}[d] + (h if it == 0 else c)
-            remote(rs_send.at[it, slot], rs_fin.at[it, landing], rs_ssem.at[it], rf_recv.at[it, landing],
-                   at_chip(d, c if it == 0 else h)).start()
+            copy = (rs_send.at[it, slot], rs_fin.at[it, landing], rs_ssem.at[it], rf_recv.at[it, landing],
+                    at_chip(d, c if it == 0 else h))
+            if abs(d) == 2:
+                start_rows(*copy)
+            else:
+                remote(*copy).start()
 
         def came(landing):
             wait_recv(rs_in.at[it, landing], rs_recv.at[it, landing])
@@ -398,7 +408,7 @@
         part = gat.at[1, y * 2 + h]
         part[...] = p.astype(BF16)
         for d in (2, -2):
-            remote(part, part, ag_send.at[1], ag_recv.at[1, y * 2 + h], at_chip(d, c)).start()
+            start_rows(part, part, ag_send.at[1], ag_recv.at[1, y * 2 + h], at_chip(d, c))
     for h in range(2):
         part = gat.at[1, y * 2 + h]
         for d in (1, -1):

time: 77.2 us -> 77.3 us (level)
  no operation moved by 1% of the time
where the time goes in v13:
time: 77.3 us; the launch traced here: 77.1 us
  Pallas kernels  75.2 us (97%)
  local copies, waits for them, and re-layouts  1.28 us (2%)
    pallas_call x1, Pallas kernels, shards(): pl.pallas_call(kernel, out_shape=(out, out), in_specs=[pl.BlockSpec(memor...  75.2 us

profile of v13, /device:TPU:1, one launch (start us, length us, event | category | flops | bytes accessed | tf_op | source)
XLA Modules:
  0.0 77.1 jit_solution(553933649424888213)
XLA Ops:
  0.6 75.2 %shard_map.77 = (f32[48,2,256]{2,1,0:T(2,128)S(1)}, f32[48,2,256]{2,1,0:T(2,128)S(1)}) custom-call(bf16[2,4096,128]{2,1,0:T(8,128)(2,1)} %k_hbm.1, f32[48,2,256]{2,1,0:T(2,128)} %g_hbm.1, f32[48,2,128]{2,1,0:T(2,128)} %tr_hbm.1, f32[48,128]{1,0:T(8,128)} %op_hbm.1, s32[48,128]{1,0:T(8,128)} %st_hbm.1, s32[1,128]{1,0:T(1,128)} %bitcast.1), custom_call_target="tpu_custom_call" | custom-call | flops 805306368 | bytes 4194304 | tf_op jit(solution)/shard_map/pallas_call | solution.py:463
  75.8 0.6 copy.10
  76.5 0.6 copy.11
